TPU v7x, 512 devices: a whole 4x4x16 slice. The times are simulated.
512 devices in a mesh: ctx: 128 (over z, y, core), head: 4 (over x).
Axes of the slice: x: 4, y: 4, z: 16, core: 2. Of those that a mesh axis runs over, the one named last changes fastest.
Arguments:
- queries: bfloat16 [32768, 12288], P(('ctx', 'head')), may hold values from -96 to 96
- key_rows: bfloat16 [32768, 768], P(('ctx', 'head')), may hold values from -8 to 8
- values: bfloat16 [32768, 512], P(('ctx', 'head')), may hold values from -6 to 6
- gate_logits: bfloat16 [32768, 128], P(('ctx', 'head')), may hold values from -6 to 6
- key_mix: bfloat16 [4, 32, 192], replicated, may hold values from -1 to 1
- key_proj: bfloat16 [4, 192, 192], replicated, may hold values from -1 to 1
- value_mix: bfloat16 [4, 32, 128], replicated, may hold values from -1 to 1
- value_proj: bfloat16 [4, 128, 128], replicated, may hold values from -0.5 to 0.5
Outputs:
- mixture: bfloat16 [32768, 8192], P(('ctx', 'head'))
All inputs are finite; a program needn't handle non-finite values.
Results may differ from a plain program's by a relative error of at most 0.012.
Values may be sent and summed in bfloat16 or wider, within the bound.
A program may use at most 64 MiB of HBM per device.

v0:
```python
import math

import jax
import jax.numpy as jnp
from jax import lax
from jax.sharding import PartitionSpec as P

QHEADS = 64
GROUPS = 4
KDIM = 192
VDIM = 128
BLOCK = 32
STRIDE = 16
WINDOW = 512


def passed_along(value, axis, steps):
    count = lax.axis_size(axis)
    leading, last = (max(0, -steps), min(count, count - steps))
    return lax.ppermute(value, axis, [(source, source + steps) for source in range(leading, last)])


def compress_block(rows, mixer, projection):
    block_count = rows.shape[0] // STRIDE - 1
    halves = rows.reshape(block_count + 1, STRIDE, rows.shape[1], rows.shape[2])
    pooled = jnp.einsum(
        "bjgd,gjd->bgd", halves[:-1], mixer[:, :STRIDE], preferred_element_type=jnp.float32
    )
    pooled = pooled + jnp.einsum(
        "bjgd,gjd->bgd", halves[1:], mixer[:, STRIDE:], preferred_element_type=jnp.float32
    )
    summary = jnp.einsum(
        "bgd,gde->bge", pooled.astype(jnp.bfloat16), projection, preferred_element_type=jnp.float32
    )
    return summary.astype(jnp.bfloat16)


def soft_mix(scores, visible, value_rows):
    masked = jnp.where(visible, scores, -1e30)
    highest = jnp.max(masked, axis=-1, keepdims=True)
    weights = jnp.where(visible, jnp.exp(scores - highest), 0.0)
    weight_total = jnp.sum(weights, axis=-1)
    numerator = jnp.einsum(
        "tghs,sgd->tghd",
        weights.astype(jnp.bfloat16),
        value_rows,
        preferred_element_type=jnp.float32,
    )
    safe_total = jnp.where(weight_total > 0.0, weight_total, 1.0)
    return numerator / safe_total[..., None]


def attend(
    query_rows,
    own_keys,
    own_values,
    gate_rows,
    key_mix,
    key_proj,
    value_mix,
    value_proj,
    group_count,
    query_offset,
):
    per_group = QHEADS // GROUPS
    row_count = query_rows.shape[0]
    block_rows = own_keys.shape[0]
    score_scale = 1.0 / math.sqrt(KDIM)
    queried = query_rows.reshape(row_count, group_count, per_group, KDIM)
    block_keys = own_keys.reshape(block_rows, group_count, KDIM)
    block_values = own_values.reshape(block_rows, group_count, VDIM)
    block_first = lax.axis_index("ctx") * block_rows
    positions = block_first + query_offset + jnp.arange(row_count, dtype=jnp.int32)
    next_keys, next_values = passed_along((block_keys[:STRIDE], block_values[:STRIDE]), "ctx", -1)
    summary_keys = compress_block(jnp.concatenate([block_keys, next_keys], 0), key_mix, key_proj)
    summary_values = compress_block(
        jnp.concatenate([block_values, next_values], 0), value_mix, value_proj
    )
    distance_count = -(-WINDOW // block_rows)
    near_keys = []
    near_values = []
    for distance in range(distance_count, 0, -1):
        far_keys, far_values = passed_along((block_keys, block_values), "ctx", distance)
        near_keys.append(far_keys)
        near_values.append(far_values)
    near_keys.append(block_keys)
    near_values.append(block_values)
    near_keys = jnp.concatenate(near_keys, 0)
    near_values = jnp.concatenate(near_values, 0)
    key_places = (
        block_first - distance_count * block_rows + jnp.arange(near_keys.shape[0], dtype=jnp.int32)
    )
    near_visible = (
        (key_places[None, :] <= positions[:, None])
        & (key_places[None, :] > positions[:, None] - WINDOW)
        & (key_places[None, :] >= 0)
    )
    scores = (
        jnp.einsum("tghd,sgd->tghs", queried, near_keys, preferred_element_type=jnp.float32)
        * score_scale
    )
    window_out = soft_mix(scores, near_visible[:, None, None, :], near_values)

    def absorb_part(running, portion, offset):
        part_keys, part_values = portion
        block_ends = (offset + jnp.arange(part_keys.shape[0], dtype=jnp.int32)) * STRIDE + BLOCK - 1
        visible = (block_ends[None, :] <= positions[:, None])[:, None, None, :]
        highest, weight_total, numerator = running
        part_scores = (
            jnp.einsum("tghd,bgd->tghb", queried, part_keys, preferred_element_type=jnp.float32)
            * score_scale
        )
        masked = jnp.where(visible, part_scores, -1e30)
        new_highest = jnp.maximum(highest, jnp.max(masked, axis=-1))
        weights = jnp.where(visible, jnp.exp(part_scores - new_highest[..., None]), 0.0)
        factor = jnp.exp(highest - new_highest)
        weight_total = weight_total * factor + jnp.sum(weights, axis=-1)
        numerator = numerator * factor[..., None] + jnp.einsum(
            "tghb,bgd->tghd",
            weights.astype(jnp.bfloat16),
            part_values,
            preferred_element_type=jnp.float32,
        )
        return (new_highest, weight_total, numerator)

    initial = (
        jnp.full((row_count, group_count, per_group), -1e30, jnp.float32),
        jnp.zeros((row_count, group_count, per_group), jnp.float32),
        jnp.zeros((row_count, group_count, per_group, VDIM), jnp.float32),
    )
    portion = (
        lax.all_gather(summary_keys, "ctx", axis=0, tiled=True),
        lax.all_gather(summary_values, "ctx", axis=0, tiled=True),
    )
    part_count = portion[0].shape[0]

    def step(step_index, state):
        sub_keys = lax.dynamic_slice_in_dim(portion[0], step_index * 256, 256, 0)
        sub_values = lax.dynamic_slice_in_dim(portion[1], step_index * 256, 256, 0)
        return absorb_part(state, (sub_keys, sub_values), step_index * 256)

    highest, weight_total, numerator = lax.fori_loop(0, part_count // 256, step, initial)
    compressed_out = numerator / jnp.where(weight_total > 0.0, weight_total, 1.0)[..., None]
    gate_values = jax.nn.sigmoid(
        gate_rows.reshape(row_count, group_count, per_group, 2).astype(jnp.float32)
    )
    mixture = gate_values[..., 0:1] * compressed_out + gate_values[..., 1:2] * window_out
    return mixture.astype(jnp.bfloat16).reshape(row_count, group_count * per_group * VDIM)


def local(queries, key_rows, values, gate_logits, key_mix, key_proj, value_mix, value_proj):
    query_rows, own_keys, own_values, gate_rows = (
        lax.all_to_all(queries, "head", split_axis=1, concat_axis=0, tiled=True),
        lax.all_to_all(key_rows, "head", split_axis=1, concat_axis=0, tiled=True),
        lax.all_to_all(values, "head", split_axis=1, concat_axis=0, tiled=True),
        lax.all_to_all(gate_logits, "head", split_axis=1, concat_axis=0, tiled=True),
    )
    group_index = lax.axis_index("head")
    key_mix = lax.dynamic_slice_in_dim(key_mix, group_index, 1, 0)
    key_proj = lax.dynamic_slice_in_dim(key_proj, group_index, 1, 0)
    value_mix = lax.dynamic_slice_in_dim(value_mix, group_index, 1, 0)
    value_proj = lax.dynamic_slice_in_dim(value_proj, group_index, 1, 0)
    group_count = 1
    query_offset = 0
    mixture = attend(
        query_rows,
        own_keys,
        own_values,
        gate_rows,
        key_mix,
        key_proj,
        value_mix,
        value_proj,
        group_count,
        query_offset,
    )
    return lax.all_to_all(mixture, "head", split_axis=0, concat_axis=1, tiled=True)


def solution(mesh):
    placed = (
        P(("ctx", "head"), None),
        P(("ctx", "head"), None),
        P(("ctx", "head"), None),
        P(("ctx", "head"), None),
        P(),
        P(),
        P(),
        P(),
    )
    return jax.shard_map(
        local, mesh=mesh, in_specs=placed, out_specs=P(("ctx", "head"), None), check_vma=False
    )
```

profile of v0, /device:TPU:1, one launch (start us, length us, event | category | flops | bytes accessed | tf_op | source)
XLA Modules:
  0.0 378.0 jit_solution(15518361057223146056)
XLA Ops:
  1.6 4.8 %all-to-all-start = ((bf16[4,2,1024]{2,1,0:T(2,128)(2,1)}), bf16[4,2,1024]{2,1,0:T(2,128)(2,1)S(1)}, u32[]{:S(2)}, u32[]{:S(2)}) async-start(bf16[4,2,1024]{2,1,0:T(2,128)(2,1)} %reshape.421), calls=%async_computation | async-start | bytes 32768 | tf_op jit(solution)/shard_map/all_to_all | solution.py:156
  14.7 4.2 %all-to-all-start.3 = ((bf16[64,4,128]{2,0,1:T(8,128)(2,1)}), bf16[64,4,128]{2,0,1:T(8,128)(2,1)S(1)}, u32[]{:S(2)}, u32[]{:S(2)}) async-start(bf16[64,4,128]{2,0,1:T(8,128)(2,1)} %copy_bitcast_fusion.1), calls=%async_computation.3 | async-start | bytes 131072 | tf_op jit(solution)/shard_map/all_to_all | solution.py:155
  19.3 4.2 %all-to-all-done.3 = bf16[64,4,128]{2,0,1:T(8,128)(2,1)S(1)} async-done(((bf16[64,4,128]{2,0,1:T(8,128)(2,1)}), bf16[64,4,128]{2,0,1:T(8,128)(2,1)S(1)}, u32[]{:S(2)}, u32[]{:S(2)}) %all-to-all-start.3) | async-done | bytes 65568 | tf_op jit(solution)/shard_map/all_to_all | solution.py:155
  28.1 3.8 %collective-permute-start.2 = (bf16[256,1,128]{0,2,1:T(8,128)(2,1)}, bf16[256,1,128]{0,2,1:T(8,128)(2,1)}, u32[]{:S(2)}, u32[]{:S(2)}) collective-permute-start(bf16[256,1,128]{0,2,1:T(8,128)(2,1)} %copy.63), channel_id=1, source_target_pairs={{0,8},{4,12},{8,16},{12,20},{16,24},{20,28},{24,32},{28,36},{32,40... | collective-permute-start | bytes 196616 | tf_op jit(solution)/shard_map/ppermute | solution.py:20
  31.9 5.4 %collective-permute-start.3 = (bf16[256,1,128]{0,2,1:T(8,128)(2,1)}, bf16[256,1,128]{0,2,1:T(8,128)(2,1)}, u32[]{:S(2)}, u32[]{:S(2)}) collective-permute-start(bf16[256,1,128]{0,2,1:T(8,128)(2,1)} %copy.63), channel_id=1, source_target_pairs={{0,4},{4,8},{8,12},{12,16},{16,20},{20,24},{24,28},{28,32},{32,36}... | collective-permute-start | bytes 196616 | tf_op jit(solution)/shard_map/ppermute | solution.py:20
  37.3 3.4 collective-permute-start.1
  40.8 4.5 %all-to-all-start.2 = ((bf16[64,4,3072]{2,0,1:T(8,128)(2,1)}), bf16[64,4,3072]{2,0,1:T(8,128)(2,1)}, u32[]{:S(2)}, u32[]{:S(2)}) async-start(bf16[64,4,3072]{2,0,1:T(8,128)(2,1)} %bitcast.225), calls=%async_computation.2 | async-start | bytes 3145728 | tf_op jit(solution)/shard_map/all_to_all | solution.py:153
  46.5 96.4 %all_gather.7 = bf16[2048,1,128]{2,0,1:T(8,128)(2,1)} all-gather(bf16[16,1,128]{2,0,1:T(8,128)(2,1)S(1)} %fusion.43), channel_id=1, replica_groups=mesh['ctx'=128,'head'=4] {'ctx'}, dimensions={0}, use_global_device_ids=true | all-gather | bytes 528384 | tf_op jit(solution)/shard_map/all_gather | solution.py:133
  153.9 102.0 %all_gather.6 = bf16[2048,1,192]{2,0,1:T(8,128)(2,1)S(1)} all-gather(bf16[16,1,192]{2,0,1:T(8,128)(2,1)S(1)} %fusion.42), channel_id=1, replica_groups=mesh['ctx'=128,'head'=4] {'ctx'}, dimensions={0}, use_global_device_ids=true | all-gather | bytes 792576 | tf_op jit(solution)/shard_map/all_gather | solution.py:132
  257.3 4.7 %reshape.391 = bf16[256,1,16,192]{3,2,0,1:T(8,128)(2,1)} reshape(bf16[4,64,3072]{2,1,0:T(8,128)(2,1)} %bitcast.28) | data formatting | bytes 3145728 | tf_op jit(solution)/shard_map/reshape | solution.py:69
  262.0 4.4 %copy.61 = bf16[256,1,16,192]{0,3,2,1:T(8,128)(2,1)} copy(bf16[256,1,16,192]{3,2,0,1:T(8,128)(2,1)} %reshape.391) | data formatting | bytes 3145728
  266.4 73.6 %while.22 = (s32[]{:T(128)}, f32[256,1,16]{0,2,1:T(8,128)S(1)}, f32[256,1,16]{0,2,1:T(8,128)S(1)}, f32[256,1,16,128]{0,3,2,1:T(8,128)S(1)}, bf16[2048,1,192]{0,2...) while((s32[]{:T(128)}, f32[256,1,16]{0,2,1:T(8,128)S(1)}, ...), condition=%wide.region_3.4_spmd.clone, body=%wide.region_0.3_spmd.clone.sunk | while | flops 684286976 | bytes 35819736 | solution.py:142
  266.5 4.3 %fusion.80 = (f32[256,16]{0,1:T(8,128)S(1)}, f32[256,256,16]{1,0,2:T(8,128)}) fusion(pred[256,256]{0,1:T(8,128)(4,1)S(1)} %broadcast_compare_fusion.3, bf16[256,1,16,192]{0,3,2,1:T(8,128)(2,1)} %get-tuple-element.451, bf16[2048,1,192]{0,2,1:T(8,128)(2,1)} %get-tuple-element.450, s32[]{:T(128)S(6)} %select_n.112), kind=kOutput, calls=%fused_computation.3.clone.1 | convolution fusion | flops 405794816 | bytes 5947396 | tf_op jit(solution)/shard_map/while/body/eval_jaxpr/tghd,bgd->tghb/dot_general | solution.py:110
  270.9 3.8 %bitcast_add_fusion.6 = f32[256,1,16,128]{0,3,2,1:T(8,128)S(1)} fusion(f32[256,1,16,128]{0,3,2,1:T(8,128)S(1)} %get-tuple-element.437, f32[256,256,16]{1,0,2:T(8,128)} %get-tuple-element.420, f32[256,16]{0,1:T(8,128)S(1)} %bitcast.223, pred[256,256]{0,1:T(8,128)(4,1)S(1)} %broadcast_compare_fusion.3, f32[256,16]{0,1:T(8,128)S(1)} %get-tuple-element.421, ...), kind=kOutput, calls=%fused_computation.10.clone.1 | convolution fusion | flops 274202624 | bytes 8552453 | tf_op jit(solution)/shard_map/while/body/eval_jaxpr/tghb,bgd->tghd/dot_general | solution.py:118
  275.8 4.3 %fusion.80 = (f32[256,16]{0,1:T(8,128)S(1)}, f32[256,256,16]{1,0,2:T(8,128)}) fusion(pred[256,256]{0,1:T(8,128)(4,1)S(1)} %broadcast_compare_fusion.3, bf16[256,1,16,192]{0,3,2,1:T(8,128)(2,1)} %get-tuple-element.451, bf16[2048,1,192]{0,2,1:T(8,128)(2,1)} %get-tuple-element.450, s32[]{:T(128)S(6)} %select_n.112), kind=kOutput, calls=%fused_computation.3.clone.1 | convolution fusion | flops 405794816 | bytes 5947396 | tf_op jit(solution)/shard_map/while/body/eval_jaxpr/tghd,bgd->tghb/dot_general | solution.py:110
  280.1 3.8 %bitcast_add_fusion.6 = f32[256,1,16,128]{0,3,2,1:T(8,128)S(1)} fusion(f32[256,1,16,128]{0,3,2,1:T(8,128)S(1)} %get-tuple-element.437, f32[256,256,16]{1,0,2:T(8,128)} %get-tuple-element.420, f32[256,16]{0,1:T(8,128)S(1)} %bitcast.223, pred[256,256]{0,1:T(8,128)(4,1)S(1)} %broadcast_compare_fusion.3, f32[256,16]{0,1:T(8,128)S(1)} %get-tuple-element.421, ...), kind=kOutput, calls=%fused_computation.10.clone.1 | convolution fusion | flops 274202624 | bytes 8552453 | tf_op jit(solution)/shard_map/while/body/eval_jaxpr/tghb,bgd->tghd/dot_general | solution.py:118
  285.0 4.3 %fusion.80 = (f32[256,16]{0,1:T(8,128)S(1)}, f32[256,256,16]{1,0,2:T(8,128)}) fusion(pred[256,256]{0,1:T(8,128)(4,1)S(1)} %broadcast_compare_fusion.3, bf16[256,1,16,192]{0,3,2,1:T(8,128)(2,1)} %get-tuple-element.451, bf16[2048,1,192]{0,2,1:T(8,128)(2,1)} %get-tuple-element.450, s32[]{:T(128)S(6)} %select_n.112), kind=kOutput, calls=%fused_computation.3.clone.1 | convolution fusion | flops 405794816 | bytes 5947396 | tf_op jit(solution)/shard_map/while/body/eval_jaxpr/tghd,bgd->tghb/dot_general | solution.py:110
  289.3 3.8 %bitcast_add_fusion.6 = f32[256,1,16,128]{0,3,2,1:T(8,128)S(1)} fusion(f32[256,1,16,128]{0,3,2,1:T(8,128)S(1)} %get-tuple-element.437, f32[256,256,16]{1,0,2:T(8,128)} %get-tuple-element.420, f32[256,16]{0,1:T(8,128)S(1)} %bitcast.223, pred[256,256]{0,1:T(8,128)(4,1)S(1)} %broadcast_compare_fusion.3, f32[256,16]{0,1:T(8,128)S(1)} %get-tuple-element.421, ...), kind=kOutput, calls=%fused_computation.10.clone.1 | convolution fusion | flops 274202624 | bytes 8552453 | tf_op jit(solution)/shard_map/while/body/eval_jaxpr/tghb,bgd->tghd/dot_general | solution.py:118
  294.2 4.3 %fusion.80 = (f32[256,16]{0,1:T(8,128)S(1)}, f32[256,256,16]{1,0,2:T(8,128)}) fusion(pred[256,256]{0,1:T(8,128)(4,1)S(1)} %broadcast_compare_fusion.3, bf16[256,1,16,192]{0,3,2,1:T(8,128)(2,1)} %get-tuple-element.451, bf16[2048,1,192]{0,2,1:T(8,128)(2,1)} %get-tuple-element.450, s32[]{:T(128)S(6)} %select_n.112), kind=kOutput, calls=%fused_computation.3.clone.1 | convolution fusion | flops 405794816 | bytes 5947396 | tf_op jit(solution)/shard_map/while/body/eval_jaxpr/tghd,bgd->tghb/dot_general | solution.py:110
  298.5 3.8 %bitcast_add_fusion.6 = f32[256,1,16,128]{0,3,2,1:T(8,128)S(1)} fusion(f32[256,1,16,128]{0,3,2,1:T(8,128)S(1)} %get-tuple-element.437, f32[256,256,16]{1,0,2:T(8,128)} %get-tuple-element.420, f32[256,16]{0,1:T(8,128)S(1)} %bitcast.223, pred[256,256]{0,1:T(8,128)(4,1)S(1)} %broadcast_compare_fusion.3, f32[256,16]{0,1:T(8,128)S(1)} %get-tuple-element.421, ...), kind=kOutput, calls=%fused_computation.10.clone.1 | convolution fusion | flops 274202624 | bytes 8552453 | tf_op jit(solution)/shard_map/while/body/eval_jaxpr/tghb,bgd->tghd/dot_general | solution.py:118
  303.4 4.3 %fusion.80 = (f32[256,16]{0,1:T(8,128)S(1)}, f32[256,256,16]{1,0,2:T(8,128)}) fusion(pred[256,256]{0,1:T(8,128)(4,1)S(1)} %broadcast_compare_fusion.3, bf16[256,1,16,192]{0,3,2,1:T(8,128)(2,1)} %get-tuple-element.451, bf16[2048,1,192]{0,2,1:T(8,128)(2,1)} %get-tuple-element.450, s32[]{:T(128)S(6)} %select_n.112), kind=kOutput, calls=%fused_computation.3.clone.1 | convolution fusion | flops 405794816 | bytes 5947396 | tf_op jit(solution)/shard_map/while/body/eval_jaxpr/tghd,bgd->tghb/dot_general | solution.py:110
  307.7 3.8 %bitcast_add_fusion.6 = f32[256,1,16,128]{0,3,2,1:T(8,128)S(1)} fusion(f32[256,1,16,128]{0,3,2,1:T(8,128)S(1)} %get-tuple-element.437, f32[256,256,16]{1,0,2:T(8,128)} %get-tuple-element.420, f32[256,16]{0,1:T(8,128)S(1)} %bitcast.223, pred[256,256]{0,1:T(8,128)(4,1)S(1)} %broadcast_compare_fusion.3, f32[256,16]{0,1:T(8,128)S(1)} %get-tuple-element.421, ...), kind=kOutput, calls=%fused_computation.10.clone.1 | convolution fusion | flops 274202624 | bytes 8552453 | tf_op jit(solution)/shard_map/while/body/eval_jaxpr/tghb,bgd->tghd/dot_general | solution.py:118
  312.6 4.3 %fusion.80 = (f32[256,16]{0,1:T(8,128)S(1)}, f32[256,256,16]{1,0,2:T(8,128)}) fusion(pred[256,256]{0,1:T(8,128)(4,1)S(1)} %broadcast_compare_fusion.3, bf16[256,1,16,192]{0,3,2,1:T(8,128)(2,1)} %get-tuple-element.451, bf16[2048,1,192]{0,2,1:T(8,128)(2,1)} %get-tuple-element.450, s32[]{:T(128)S(6)} %select_n.112), kind=kOutput, calls=%fused_computation.3.clone.1 | convolution fusion | flops 405794816 | bytes 5947396 | tf_op jit(solution)/shard_map/while/body/eval_jaxpr/tghd,bgd->tghb/dot_general | solution.py:110
  316.9 3.8 %bitcast_add_fusion.6 = f32[256,1,16,128]{0,3,2,1:T(8,128)S(1)} fusion(f32[256,1,16,128]{0,3,2,1:T(8,128)S(1)} %get-tuple-element.437, f32[256,256,16]{1,0,2:T(8,128)} %get-tuple-element.420, f32[256,16]{0,1:T(8,128)S(1)} %bitcast.223, pred[256,256]{0,1:T(8,128)(4,1)S(1)} %broadcast_compare_fusion.3, f32[256,16]{0,1:T(8,128)S(1)} %get-tuple-element.421, ...), kind=kOutput, calls=%fused_computation.10.clone.1 | convolution fusion | flops 274202624 | bytes 8552453 | tf_op jit(solution)/shard_map/while/body/eval_jaxpr/tghb,bgd->tghd/dot_general | solution.py:118
  321.8 4.3 %fusion.80 = (f32[256,16]{0,1:T(8,128)S(1)}, f32[256,256,16]{1,0,2:T(8,128)}) fusion(pred[256,256]{0,1:T(8,128)(4,1)S(1)} %broadcast_compare_fusion.3, bf16[256,1,16,192]{0,3,2,1:T(8,128)(2,1)} %get-tuple-element.451, bf16[2048,1,192]{0,2,1:T(8,128)(2,1)} %get-tuple-element.450, s32[]{:T(128)S(6)} %select_n.112), kind=kOutput, calls=%fused_computation.3.clone.1 | convolution fusion | flops 405794816 | bytes 5947396 | tf_op jit(solution)/shard_map/while/body/eval_jaxpr/tghd,bgd->tghb/dot_general | solution.py:110
  326.1 3.8 %bitcast_add_fusion.6 = f32[256,1,16,128]{0,3,2,1:T(8,128)S(1)} fusion(f32[256,1,16,128]{0,3,2,1:T(8,128)S(1)} %get-tuple-element.437, f32[256,256,16]{1,0,2:T(8,128)} %get-tuple-element.420, f32[256,16]{0,1:T(8,128)S(1)} %bitcast.223, pred[256,256]{0,1:T(8,128)(4,1)S(1)} %broadcast_compare_fusion.3, f32[256,16]{0,1:T(8,128)S(1)} %get-tuple-element.421, ...), kind=kOutput, calls=%fused_computation.10.clone.1 | convolution fusion | flops 274202624 | bytes 8552453 | tf_op jit(solution)/shard_map/while/body/eval_jaxpr/tghb,bgd->tghd/dot_general | solution.py:118
  331.0 4.3 %fusion.80 = (f32[256,16]{0,1:T(8,128)S(1)}, f32[256,256,16]{1,0,2:T(8,128)}) fusion(pred[256,256]{0,1:T(8,128)(4,1)S(1)} %broadcast_compare_fusion.3, bf16[256,1,16,192]{0,3,2,1:T(8,128)(2,1)} %get-tuple-element.451, bf16[2048,1,192]{0,2,1:T(8,128)(2,1)} %get-tuple-element.450, s32[]{:T(128)S(6)} %select_n.112), kind=kOutput, calls=%fused_computation.3.clone.1 | convolution fusion | flops 405794816 | bytes 5947396 | tf_op jit(solution)/shard_map/while/body/eval_jaxpr/tghd,bgd->tghb/dot_general | solution.py:110
  335.3 3.8 %bitcast_add_fusion.6 = f32[256,1,16,128]{0,3,2,1:T(8,128)S(1)} fusion(f32[256,1,16,128]{0,3,2,1:T(8,128)S(1)} %get-tuple-element.437, f32[256,256,16]{1,0,2:T(8,128)} %get-tuple-element.420, f32[256,16]{0,1:T(8,128)S(1)} %bitcast.223, pred[256,256]{0,1:T(8,128)(4,1)S(1)} %broadcast_compare_fusion.3, f32[256,16]{0,1:T(8,128)S(1)} %get-tuple-element.421, ...), kind=kOutput, calls=%fused_computation.10.clone.1 | convolution fusion | flops 274202624 | bytes 8552453 | tf_op jit(solution)/shard_map/while/body/eval_jaxpr/tghb,bgd->tghd/dot_general | solution.py:118
  340.1 4.7 %reshape.401 = bf16[256,16,192]{2,1,0:T(8,128)(2,1)} reshape(bf16[4,64,3072]{2,1,0:T(8,128)(2,1)} %bitcast.28) | data formatting | bytes 3145728 | tf_op jit(solution)/shard_map/reshape.38
  344.8 4.7 %fusion.27 = (f32[256,16]{0,1:T(8,128)S(1)}, f32[768,256,16]{1,0,2:T(8,128)S(1)}) fusion(pred[256,768]{0,1:T(8,128)(4,1)S(1)} %copy-done.2, bf16[256,16,192]{2,1,0:T(8,128)(2,1)} %reshape.401, bf16[256,1,192]{0,2,1:T(8,128)(2,1)} %copy.66, bf16[256,1,192]{0,2,1:T(8,128)(2,1)} %collective-permute-done.5, bf16[256,1,192]{0,2,1:T(8,128)(2,1)} %collective-permute-done.4), kind=kOutput, calls=%fused_computation.36 | convolution fusion | flops 1218277376 | bytes 14663680 | tf_op jit(solution)/shard_map/tghd,sgd->tghs/dot_general | solution.py:99
  352.1 3.9 %fusion.36 = bf16[256,1,16,128]{0,3,2,1:T(8,128)(2,1)S(1)} fusion(f32[256,1,16,128]{0,3,2,1:T(8,128)S(1)} %get-tuple-element.263, f32[768,256,16]{1,0,2:T(8,128)S(1)} %get-tuple-element.356, f32[256,16]{0,1:T(8,128)S(1)} %get-tuple-element.355, pred[256,768]{0,1:T(8,128)(4,1)S(1)} %copy-done.3, f32[256,16]{0,1:T(8,128)S(1)} %compare_select_fusion, ...), kind=kOutput, calls=%fused_computation.45 | convolution fusion | flops 821624832 | bytes 16203776 | tf_op jit(solution)/shard_map/tghs,sgd->tghd/dot_general | solution.py:43
  357.7 19.2 %all_to_all.80 = bf16[4,64,2048]{2,1,0:T(8,128)(2,1)S(1)} all-to-all(bf16[4,64,2048]{2,1,0:T(8,128)(2,1)S(1)} %all_to_all.71), channel_id=1, replica_groups=mesh['ctx'=128,'head'=4] {'head'}, dimensions={0} | all-to-all | bytes 2097152 | tf_op jit(solution)/shard_map/all_to_all | solution.py:177
  (133 shorter events, 41.6 us)
Async XLA Ops:
  0.0 153.7 %copy-start = (bf16[4,192,192]{2,1,0:T(8,128)(2,1)S(1)}, bf16[4,192,192]{2,1,0:T(8,128)(2,1)}, u32[]{:S(2)}) copy-start(bf16[4,192,192]{2,1,0:T(8,128)(2,1)} %param.15) | copy-start | bytes 884740
  1.6 13.1 %all-to-all-start = ((bf16[4,2,1024]{2,1,0:T(2,128)(2,1)}), bf16[4,2,1024]{2,1,0:T(2,128)(2,1)S(1)}, u32[]{:S(2)}, u32[]{:S(2)}) async-start(bf16[4,2,1024]{2,1,0:T(2,128)(2,1)} %reshape.421), calls=%async_computation | async-start | bytes 32768 | tf_op jit(solution)/shard_map/all_to_all | solution.py:156
  14.7 8.7 %all-to-all-start.3 = ((bf16[64,4,128]{2,0,1:T(8,128)(2,1)}), bf16[64,4,128]{2,0,1:T(8,128)(2,1)S(1)}, u32[]{:S(2)}, u32[]{:S(2)}) async-start(bf16[64,4,128]{2,0,1:T(8,128)(2,1)} %copy_bitcast_fusion.1), calls=%async_computation.3 | async-start | bytes 131072 | tf_op jit(solution)/shard_map/all_to_all | solution.py:155
  23.4 17.3 %all-to-all-start.1 = ((bf16[64,4,192]{2,0,1:T(8,128)(2,1)}), bf16[64,4,192]{2,0,1:T(8,128)(2,1)S(1)}, u32[]{:S(2)}, u32[]{:S(2)}) async-start(bf16[64,4,192]{2,0,1:T(8,128)(2,1)} %copy.57), calls=%async_computation.1 | async-start | bytes 262144 | tf_op jit(solution)/shard_map/all_to_all | solution.py:154
  28.1 324.0 %collective-permute-start.2 = (bf16[256,1,128]{0,2,1:T(8,128)(2,1)}, bf16[256,1,128]{0,2,1:T(8,128)(2,1)}, u32[]{:S(2)}, u32[]{:S(2)}) collective-permute-start(bf16[256,1,128]{0,2,1:T(8,128)(2,1)} %copy.63), channel_id=1, source_target_pairs={{0,8},{4,12},{8,16},{12,20},{16,24},{20,28},{24,32},{28,36},{32,40... | collective-permute-start | bytes 196616 | tf_op jit(solution)/shard_map/ppermute | solution.py:20
  31.9 320.2 %collective-permute-start.3 = (bf16[256,1,128]{0,2,1:T(8,128)(2,1)}, bf16[256,1,128]{0,2,1:T(8,128)(2,1)}, u32[]{:S(2)}, u32[]{:S(2)}) collective-permute-start(bf16[256,1,128]{0,2,1:T(8,128)(2,1)} %copy.63), channel_id=1, source_target_pairs={{0,4},{4,8},{8,12},{12,16},{16,20},{20,24},{24,28},{28,32},{32,36}... | collective-permute-start | bytes 196616 | tf_op jit(solution)/shard_map/ppermute | solution.py:20
  37.3 8.1 %collective-permute-start.1 = (bf16[16,1,128]{2,0,1:T(8,128)(2,1)S(1)}, bf16[16,1,128]{2,0,1:T(8,128)(2,1)S(1)}, u32[]{:S(2)}, u32[]{:S(2)}) collective-permute-start(bf16[16,1,128]{2,0,1:T(8,128)(2,1)S(1)} %slice.48), channel_id=1, source_target_pairs={{4,0},{8,4},{12,8},{16,12},{20,16},{24,20},{28,24},{32,28},{36,32}... | collective-permute-start | bytes 12296 | tf_op jit(solution)/shard_map/ppermute | solution.py:20
  40.8 216.5 %all-to-all-start.2 = ((bf16[64,4,3072]{2,0,1:T(8,128)(2,1)}), bf16[64,4,3072]{2,0,1:T(8,128)(2,1)}, u32[]{:S(2)}, u32[]{:S(2)}) async-start(bf16[64,4,3072]{2,0,1:T(8,128)(2,1)} %bitcast.225), calls=%async_computation.2 | async-start | bytes 3145728 | tf_op jit(solution)/shard_map/all_to_all | solution.py:153
  143.6 201.2 %collective-permute-start.4 = (bf16[256,1,192]{0,2,1:T(8,128)(2,1)}, bf16[256,1,192]{0,2,1:T(8,128)(2,1)}, u32[]{:S(2)}, u32[]{:S(2)}) collective-permute-start(bf16[256,1,192]{0,2,1:T(8,128)(2,1)} %copy.66), channel_id=1, source_target_pairs={{0,8},{4,12},{8,16},{12,20},{16,24},{20,28},{24,32},{28,36},{32,40... | collective-permute-start | bytes 294920 | tf_op jit(solution)/shard_map/ppermute | solution.py:20
  145.7 199.1 %collective-permute-start.5 = (bf16[256,1,192]{0,2,1:T(8,128)(2,1)}, bf16[256,1,192]{0,2,1:T(8,128)(2,1)}, u32[]{:S(2)}, u32[]{:S(2)}) collective-permute-start(bf16[256,1,192]{0,2,1:T(8,128)(2,1)} %copy.66), channel_id=1, source_target_pairs={{0,4},{4,8},{8,12},{12,16},{16,20},{20,24},{24,28},{28,32},{32,36}... | collective-permute-start | bytes 294920 | tf_op jit(solution)/shard_map/ppermute | solution.py:20
  148.5 5.0 %collective-permute-start = (bf16[16,1,192]{2,0,1:T(8,128)(2,1)S(1)}, bf16[16,1,192]{2,0,1:T(8,128)(2,1)S(1)}, u32[]{:S(2)}, u32[]{:S(2)}) collective-permute-start(bf16[16,1,192]{2,0,1:T(8,128)(2,1)S(1)} %slice.47), channel_id=1, source_target_pairs={{4,0},{8,4},{12,8},{16,12},{20,16},{24,20},{28,24},{32,28},{36,32}... | collective-permute-start | bytes 18440 | tf_op jit(solution)/shard_map/ppermute | solution.py:20
  257.3 9.1 %copy-start.4 = (f32[256,1,16]{0,2,1:T(8,128)S(1)}, f32[256,1,16]{0,2,1:T(8,128)}, u32[]{:S(2)}) copy-start(f32[256,1,16]{0,2,1:T(8,128)} %custom-call.1) | copy-start | bytes 49156
  266.4 78.4 %copy-start.2 = (pred[256,768]{0,1:T(8,128)(4,1)S(1)}, pred[256,768]{0,1:T(8,128)(4,1)}, u32[]{:S(2)}) copy-start(pred[256,768]{0,1:T(8,128)(4,1)} %and_and_fusion) | copy-start | bytes 589828
  270.8 3.8 %copy-start.1 = (f32[256,256,16]{1,0,2:T(8,128)S(1)}, f32[256,256,16]{1,0,2:T(8,128)}, u32[]{:S(2)}) copy-start(f32[256,256,16]{1,0,2:T(8,128)} %get-tuple-element.420) | copy-start | bytes 12582916 | tf_op jit(solution)/shard_map/while
  280.1 3.8 %copy-start.1 = (f32[256,256,16]{1,0,2:T(8,128)S(1)}, f32[256,256,16]{1,0,2:T(8,128)}, u32[]{:S(2)}) copy-start(f32[256,256,16]{1,0,2:T(8,128)} %get-tuple-element.420) | copy-start | bytes 12582916 | tf_op jit(solution)/shard_map/while
  289.3 3.8 %copy-start.1 = (f32[256,256,16]{1,0,2:T(8,128)S(1)}, f32[256,256,16]{1,0,2:T(8,128)}, u32[]{:S(2)}) copy-start(f32[256,256,16]{1,0,2:T(8,128)} %get-tuple-element.420) | copy-start | bytes 12582916 | tf_op jit(solution)/shard_map/while
  298.5 3.8 %copy-start.1 = (f32[256,256,16]{1,0,2:T(8,128)S(1)}, f32[256,256,16]{1,0,2:T(8,128)}, u32[]{:S(2)}) copy-start(f32[256,256,16]{1,0,2:T(8,128)} %get-tuple-element.420) | copy-start | bytes 12582916 | tf_op jit(solution)/shard_map/while
  307.7 3.8 %copy-start.1 = (f32[256,256,16]{1,0,2:T(8,128)S(1)}, f32[256,256,16]{1,0,2:T(8,128)}, u32[]{:S(2)}) copy-start(f32[256,256,16]{1,0,2:T(8,128)} %get-tuple-element.420) | copy-start | bytes 12582916 | tf_op jit(solution)/shard_map/while
  316.9 3.8 %copy-start.1 = (f32[256,256,16]{1,0,2:T(8,128)S(1)}, f32[256,256,16]{1,0,2:T(8,128)}, u32[]{:S(2)}) copy-start(f32[256,256,16]{1,0,2:T(8,128)} %get-tuple-element.420) | copy-start | bytes 12582916 | tf_op jit(solution)/shard_map/while
  326.1 3.8 %copy-start.1 = (f32[256,256,16]{1,0,2:T(8,128)S(1)}, f32[256,256,16]{1,0,2:T(8,128)}, u32[]{:S(2)}) copy-start(f32[256,256,16]{1,0,2:T(8,128)} %get-tuple-element.420) | copy-start | bytes 12582916 | tf_op jit(solution)/shard_map/while
  335.3 3.8 %copy-start.1 = (f32[256,256,16]{1,0,2:T(8,128)S(1)}, f32[256,256,16]{1,0,2:T(8,128)}, u32[]{:S(2)}) copy-start(f32[256,256,16]{1,0,2:T(8,128)} %get-tuple-element.420) | copy-start | bytes 12582916 | tf_op jit(solution)/shard_map/while
  349.5 2.6 copy-start.3
  349.5 2.6 copy-start.5
  349.5 2.6 copy-start.6
where the time goes:
time: 379 us; the launch traced here: 378 us
  blocking collectives  218 us (58%)
  matrix products  74.6 us (20%)
  starting transfers between devices  36.6 us (10%)
  local copies, waits for them, and re-layouts  28.1 us (7%)
  other arithmetic  13.2 us (3%)
  waiting for transfers between devices  6.88 us (2%)
    all_gather x1, blocking collectives, attend(): lax.all_gather(summary_keys, 'ctx', axis=0, tiled=True)  102 us
    all_gather x1, blocking collectives, attend(): lax.all_gather(summary_values, 'ctx', axis=0, tiled=True)  96.4 us
    dot_general x8, matrix products, absorb_part(): jnp.einsum('tghd,bgd->tghb', queried, part_keys, preferred_element_type=j...  34.3 us
    dot_general x8, matrix products, absorb_part(): jnp.einsum('tghb,bgd->tghd', weights.astype(jnp.bfloat16), part_values, p...  30.6 us
    ppermute x6, starting transfers between devices, passed_along(): lax.ppermute(value, axis, [(source, source + steps) for source in range(l...  19.7 us
    all_to_all x1, blocking collectives, local(): lax.all_to_all(mixture, 'head', split_axis=0, concat_axis=1, tiled=True)  19.2 us
    unnamed x18, local copies, waits for them, and re-layouts  8.06 us
  transfers between devices with their start and end apart: 10, of which 2 were waited for; matrix products, arithmetic and copies ran while one was open for 28% of the time, Pallas kernels for 0%

commit v1 on v0

v1 whole, which is shorter than its diff:
```python
import functools
import math

import jax
import jax.numpy as jnp
from jax import lax
from jax.experimental import pallas as pl
from jax.experimental.pallas import tpu as pltpu
from jax.sharding import PartitionSpec as P

BF = jnp.bfloat16
F32 = jnp.float32
MESH = pl.DeviceIdType.MESH
UNITS = 512
SCALE = 1.0 / math.sqrt(192.0)
NEG = -1e30


def where_am_i():
    ctx = lax.axis_index("ctx")
    x = lax.axis_index("head")
    z = ctx // 8
    y = (ctx // 2) % 4
    c = ctx % 2
    return ctx, x, z, y, c


def comm_kernel(
    kr, vr, kmix, kproj, vmix, vproj,
    win, comp,
    own, prev, mix, quad, col, zero,
    prev_s, prev_r, win_s, win_r, own_sem, quad_s, quad_r, z_s, z_r,
    a_s, a_r, b_s, b_r, d_s, d_r, loc_sem, zero_sem,
):
    ctx, x, z, y, c = where_am_i()
    unit = ctx * 4 + x
    par = x % 2
    half = x // 2
    group = 2 * c + par
    plane_base = z * 8

    def dev(v):
        return (v // 4, v % 4)

    ahead = jnp.minimum(8, UNITS - 1 - unit)
    behind = jnp.minimum(8, unit)

    barrier = pltpu.get_barrier_semaphore()

    def greet(device):
        pl.semaphore_signal(barrier, inc=1, device_id=device, device_id_type=MESH)

    lax.fori_loop(1, behind + 1, lambda d, k: (greet(dev(unit - d)), k)[1], 0)
    for m in range(1, 4):
        greet((ctx - c + (c + m // 2) % 2, x - par + (par + m % 2) % 2))
        greet((ctx, (x + m) % 4))
        greet((plane_base + ((y + m) % 4) * 2 + c, x))
    lax.fori_loop(0, z, lambda zz, k: (greet((ctx - 8 * (z - zz), x)), k)[1], 0)

    for g in range(4):
        own[g, :, 0:192] = kr[:, 192 * g:192 * g + 192]
        own[g, :, 192:256] = jnp.ones((64, 64), BF)
        own[g, :, 256:384] = vr[:, 128 * g:128 * g + 128]
        mix[g, :, 0:192] = kmix[g].astype(F32)
        mix[g, :, 192:256] = jnp.zeros((32, 64), F32)
        mix[g, :, 256:384] = vmix[g].astype(F32)

    def clear(zz, k):
        col[zz] = jnp.zeros((16, 384), BF)
        return k

    lax.fori_loop(z + 1, 16, clear, 0)
    zero[...] = jnp.zeros_like(zero)

    pl.semaphore_wait(barrier, ahead + 9 + 15 - z)

    def prev_copy(device):
        return pltpu.make_async_remote_copy(
            src_ref=own.at[:, 48:64, :], dst_ref=prev, send_sem=prev_s, recv_sem=prev_r,
            device_id=device, device_id_type=MESH)

    @pl.when(ahead > 0)
    def _():
        prev_copy(dev(unit + 1)).start()

    def win_copy(d, device):
        return pltpu.make_async_remote_copy(
            src_ref=own, dst_ref=win.at[:, 8 - d], send_sem=win_s.at[d - 1], recv_sem=win_r.at[d - 1],
            device_id=device, device_id_type=MESH)

    lax.fori_loop(1, ahead + 1, lambda d, k: (win_copy(d, dev(unit + d)).start(), k)[1], 0)
    own_copy = pltpu.make_async_copy(own, win.at[:, 8], own_sem)
    own_copy.start()

    def zero_copy(d):
        return pltpu.make_async_copy(zero, win.at[:, 8 - d], zero_sem.at[d - 1])

    lax.fori_loop(behind + 1, 9, lambda d, k: (zero_copy(d).start(), k)[1], 0)

    @pl.when(unit > 0)
    def _():
        prev_copy(dev(unit)).wait_recv()

    @pl.when(unit == 0)
    def _():
        prev[...] = jnp.zeros_like(prev)

    member = 2 * c + par
    row = lax.broadcasted_iota(jnp.int32, (16, 1), 0)
    mine = row // 4 == member
    lane = lax.broadcasted_iota(jnp.int32, (16, 384), 1)
    first = jnp.logical_and(unit == 0, row == 0)
    for g in range(4):
        rows = jnp.concatenate([prev[g].astype(F32), own[g].astype(F32)], 0).reshape(5, 16, 384)
        pooled = jnp.sum(rows[0:4] * mix[g, 0:16][None], axis=1)
        pooled = pooled + jnp.sum(rows[1:5] * mix[g, 16:32][None], axis=1)
        pooled = jnp.concatenate([pooled] * 4, 0)
        pooled = jnp.where(mine, pooled, 0.0).astype(BF)
        keys = jnp.dot(pooled[:, 0:192], kproj[g], preferred_element_type=F32)
        vals = jnp.dot(pooled[:, 256:384], vproj[g], preferred_element_type=F32)
        ones = jnp.where(jnp.logical_and(mine, jnp.logical_not(first)), 1.0, 0.0)
        keys = jnp.where(first, keys[1:2], keys)
        vals = jnp.where(first, 0.0, vals)
        tile = jnp.concatenate([keys, jnp.broadcast_to(ones, (16, 64)), vals], 1)
        quad[0, g] = tile.astype(BF)

    def quad_copy(g_to, m_from, device):
        return pltpu.make_async_remote_copy(
            src_ref=quad.at[0, g_to], dst_ref=quad.at[1, m_from], send_sem=quad_s.at[g_to],
            recv_sem=quad_r.at[m_from], device_id=device, device_id_type=MESH)

    for m in range(4):
        @pl.when(m != member)
        def _():
            quad_copy(m, member, (ctx - c + m // 2, x - par + m % 2)).start()
    for m in range(4):
        @pl.when(m != member)
        def _():
            quad_copy(m, m, (ctx, x)).wait_recv()
    total = quad[0, member].astype(F32)
    for m in range(4):
        total = total + jnp.where(m == member, 0.0, quad[1, m].astype(F32))
    col[z] = total.astype(BF)

    def z_copy(z_from, z_to):
        return pltpu.make_async_remote_copy(
            src_ref=col.at[z_from], dst_ref=col.at[z_from], send_sem=z_s.at[z_to],
            recv_sem=z_r.at[z_from], device_id=(z_to * 8 + y * 2 + c, x), device_id_type=MESH)

    lax.fori_loop(z + 1, 16, lambda zz, k: (z_copy(z, zz).start(), k)[1], 0)

    def z_wait(i, k):
        z_copy(z - 1 - i, z).wait_recv()
        return k

    lax.fori_loop(0, z, z_wait, 0)

    def peer_x(d):
        return (ctx, (x + d) % 4)

    def peer_y(d):
        return (plane_base + ((y + d) % 4) * 2 + c, x)

    def place(ci, g, yy, hh):
        return comp.at[g, pl.ds(4 * ci, 4), yy, hh]

    def a_copy(ci, d, yy, hh, gg):
        return pltpu.make_async_remote_copy(
            src_ref=col.at[pl.ds(4 * ci, 4)], dst_ref=place(ci, gg, yy, hh),
            send_sem=a_s.at[ci, d - 1], recv_sem=a_r.at[ci, d - 1],
            device_id=peer_x(d) if ci % 2 == 0 else peer_y(d), device_id_type=MESH)

    def from_a(ci, d):
        xx = (x + 4 - d) % 4 if ci % 2 == 0 else x
        yy = y if ci % 2 == 0 else (y + 4 - d) % 4
        return yy, xx // 2, 2 * c + xx % 2

    def b_ref(ci, xx, yy):
        if ci % 2 == 0:
            return comp.at[pl.ds(2 * c, 2), pl.ds(4 * ci, 4), yy]
        return comp.at[2 * c + xx % 2, pl.ds(4 * ci, 4), :, xx // 2]

    def b_copy(ci, d, xx, yy):
        ref = b_ref(ci, xx, yy)
        return pltpu.make_async_remote_copy(
            src_ref=ref, dst_ref=ref, send_sem=b_s.at[ci, d - 1], recv_sem=b_r.at[ci, d - 1],
            device_id=peer_y(d) if ci % 2 == 0 else peer_x(d), device_id_type=MESH)

    def d_copy(ci, cc):
        ref = comp.at[pl.ds(2 * cc, 2), pl.ds(4 * ci, 4)]
        return pltpu.make_async_remote_copy(
            src_ref=ref, dst_ref=ref, send_sem=d_s.at[ci], recv_sem=d_r.at[ci],
            device_id=(ctx - c + (1 - c), x), device_id_type=MESH)

    def own_place(ci):
        return pltpu.make_async_copy(col.at[pl.ds(4 * ci, 4)], place(ci, group, y, half), loc_sem.at[ci])

    for ci in (3, 2, 1, 0):
        @pl.when(4 * ci <= z)
        def _():
            own_place(ci).start()
            for d in (1, 3, 2):
                a_copy(ci, d, y, half, group).start()
    for ci in (3, 2, 1, 0):
        @pl.when(4 * ci <= z)
        def _():
            own_place(ci).wait()
            for d in (1, 3, 2):
                yy, hh, gg = from_a(ci, d)
                a_copy(ci, d, yy, hh, gg).wait_recv()
            for d in (1, 3, 2):
                b_copy(ci, d, x, y).start()
    for ci in (3, 2, 1, 0):
        @pl.when(4 * ci <= z)
        def _():
            for d in (1, 3, 2):
                if ci % 2 == 0:
                    b_copy(ci, d, x, (y + 4 - d) % 4).wait_recv()
                else:
                    b_copy(ci, d, (x + 4 - d) % 4, y).wait_recv()
            d_copy(ci, c).start()
    for ci in (3, 2, 1, 0):
        @pl.when(4 * ci <= z)
        def _():
            d_copy(ci, 1 - c).wait_recv()
            d_copy(ci, c).wait_send()
            for d in (1, 2, 3):
                a_copy(ci, d, y, half, group).wait_send()
                b_copy(ci, d, x, y).wait_send()

    lax.fori_loop(z + 1, 16, lambda zz, k: (z_copy(z, zz).wait_send(), k)[1], 0)
    for m in range(4):
        @pl.when(m != member)
        def _():
            quad_copy(m, member, (ctx, x)).wait_send()

    @pl.when(ahead > 0)
    def _():
        prev_copy(dev(unit)).wait_send()

    own_copy.wait()
    lax.fori_loop(behind + 1, 9, lambda d, k: (zero_copy(d).wait(), k)[1], 0)
    lax.fori_loop(1, ahead + 1, lambda d, k: (win_copy(d, dev(unit)).wait_send(), k)[1], 0)
    lax.fori_loop(1, behind + 1, lambda d, k: (win_copy(d, dev(unit)).wait_recv(), k)[1], 0)


def communicate(key_rows, values, key_mix, key_proj, value_mix, value_proj):
    dma = pltpu.SemaphoreType.DMA
    vmem = pl.BlockSpec(memory_space=pltpu.VMEM)
    return pl.pallas_call(
        comm_kernel,
        out_shape=(
            jax.ShapeDtypeStruct((4, 9, 64, 384), BF),
            jax.ShapeDtypeStruct((4, 16, 4, 2, 16, 384), BF),
        ),
        in_specs=[vmem] * 6,
        out_specs=(pl.BlockSpec(memory_space=pl.ANY), pl.BlockSpec(memory_space=pl.ANY)),
        scratch_shapes=[
            pltpu.VMEM((4, 64, 384), BF),
            pltpu.VMEM((4, 16, 384), BF),
            pltpu.VMEM((4, 32, 384), F32),
            pltpu.VMEM((2, 4, 16, 384), BF),
            pltpu.VMEM((16, 16, 384), BF),
            pltpu.VMEM((4, 64, 384), BF),
            dma, dma, dma((8,)), dma((8,)), dma, dma((4,)), dma((4,)), dma((16,)), dma((16,)),
            dma((4, 3)), dma((4, 3)), dma((4, 3)), dma((4, 3)), dma((4,)), dma((4,)), dma((4,)), dma((8,)),
        ],
        compiler_params=pltpu.CompilerParams(collective_id=0, has_side_effects=True, vmem_limit_bytes=32 * 2**20),
        cost_estimate=pl.CostEstimate(flops=10**8, bytes_accessed=10**7, transcendentals=0),
    )(key_rows, values, key_mix, key_proj, value_mix, value_proj)


RT = 512
KC = 1024


def attend_kernel(q_ref, g_ref, w_ref, c_ref, o_ref, qs, acc, mx, bw, bc, vlast):
    g = pl.program_id(0)
    ctx, x, z, y, c = where_am_i()
    unit = ctx * 4 + x
    nfull = z // 8
    lane = lax.broadcasted_iota(jnp.int32, (64, 256), 1)
    for h in range(16):
        j = h // 2
        if h % 2 == 0:
            t = q_ref[:, 384 * j:384 * j + 256]
            t = jnp.where(lane < 192, t, jnp.zeros_like(t))
        else:
            t = q_ref[:, 384 * j + 128:384 * j + 384].astype(F32)
            t = pltpu.roll(t, 192, 1)
            t = jnp.where(lane < 192, t, 0.0).astype(BF)
        qs[64 * h:64 * h + 64, :] = t

    @pl.when(g == 0)
    def _():
        i = lax.broadcasted_iota(jnp.int32, (64, 576), 0)
        k = lax.broadcasted_iota(jnp.int32, (64, 576), 1)
        seen = (k > i) & (k <= i + 512) & (k + 64 * (unit - 8) >= 0)
        bw[...] = jnp.where(seen, 0.0, NEG)
        i = lax.broadcasted_iota(jnp.int32, (64, KC), 0)
        k = lax.broadcasted_iota(jnp.int32, (64, KC), 1)
        zz = 8 * nfull + k // 128
        row = k % 128
        yy = row // 32
        hh = (row % 32) // 16
        m = (row % 16) // 4
        uu = 8 * (4 * zz + yy) + 4 * (m // 2) + 2 * hh + m % 2
        b = 4 * uu - 1 + row % 4
        seen = (16 * b + 31 <= 64 * unit + i) & (b >= 0)
        bc[...] = jnp.where(seen, 0.0, NEG)

    krow = lax.broadcasted_iota(jnp.int32, (KC, 384), 0)
    last = c_ref[0, pl.ds(pl.multiple_of(nfull * KC, KC), KC), :]
    vlast[...] = jnp.where(krow < 128 * (z % 8 + 1), last, jnp.zeros_like(last))
    sig = jax.nn.sigmoid(g_ref[...].astype(F32))
    sig = pltpu.roll(sig, lax.rem(128 - 32 * g, 128), 1)
    nh = RT // 64

    def scores(q, k):
        return lax.dot_general(q, k, (((1,), (1,)), ((), ())), preferred_element_type=F32)

    def tile(rt, carry):
        q = qs[pl.ds(pl.multiple_of(rt * RT, RT), RT), :]
        s = scores(q, w_ref[0, :, 0:256])
        s = (s.reshape(nh, 64, 576) + bw[...][None]).reshape(RT, 576)
        m = jnp.max(s, axis=1, keepdims=True)
        p = jnp.exp((s - m) * SCALE).astype(BF)
        aw = jnp.dot(p, w_ref[0, :, 128:384], preferred_element_type=F32)

        s = scores(q, vlast[:, 0:256])
        s = (s.reshape(nh, 64, KC) + bc[...][None]).reshape(RT, KC)
        m = jnp.maximum(jnp.max(s, axis=1, keepdims=True), -1e29)
        p = jnp.exp((s - m) * SCALE).astype(BF)
        acc[...] = jnp.dot(p, vlast[:, 128:384], preferred_element_type=F32)
        mx[...] = jnp.broadcast_to(m, (RT, 128))

        def step(i, k):
            rows = pl.ds(pl.multiple_of(i * KC, KC), KC)
            s = scores(q, c_ref[0, rows, 0:256])
            before = mx[:, 0:1]
            m = jnp.maximum(jnp.max(s, axis=1, keepdims=True), before)
            p = jnp.exp((s - m) * SCALE).astype(BF)
            factor = jnp.exp((before - m) * SCALE)
            acc[...] = acc[...] * factor + jnp.dot(p, c_ref[0, rows, 128:384], preferred_element_type=F32)
            mx[...] = jnp.broadcast_to(m, (RT, 128))
            return k

        lax.fori_loop(0, nfull, step, 0)
        ac = acc[...]
        lc = ac[:, 64:65]
        oc = ac[:, 128:256] / jnp.where(lc > 0.0, lc, 1.0)
        ow = aw[:, 128:256] / aw[:, 64:65]
        sg = pltpu.roll(sig, lax.rem(128 - 2 * nh * rt, 128), 1)
        for h in range(nh):
            r = slice(64 * h, 64 * h + 64)
            o = sg[:, 2 * h:2 * h + 1] * oc[r] + sg[:, 2 * h + 1:2 * h + 2] * ow[r]
            o_ref[:, pl.ds(pl.multiple_of((rt * nh + h) * 128, 128), 128)] = o.astype(BF)
        return carry

    lax.fori_loop(0, 1024 // RT, tile, 0)


def attend(queries, gates, win, comp):
    return pl.pallas_call(
        attend_kernel,
        grid=(4,),
        in_specs=[
            pl.BlockSpec((64, 3072), lambda g: (0, g)),
            pl.BlockSpec((64, 128), lambda g: (0, 0)),
            pl.BlockSpec((1, 576, 384), lambda g: (g, 0, 0)),
            pl.BlockSpec((1, 2048, 384), lambda g: (g, 0, 0)),
        ],
        out_specs=pl.BlockSpec((64, 2048), lambda g: (0, g)),
        out_shape=jax.ShapeDtypeStruct((64, 8192), BF),
        scratch_shapes=[
            pltpu.VMEM((1024, 256), BF), pltpu.VMEM((RT, 256), F32), pltpu.VMEM((RT, 128), F32),
            pltpu.VMEM((64, 576), F32), pltpu.VMEM((64, KC), F32), pltpu.VMEM((KC, 384), BF),
        ],
        compiler_params=pltpu.CompilerParams(vmem_limit_bytes=48 * 2**20),
    )(queries, gates, win, comp)


def local(queries, key_rows, values, gate_logits, key_mix, key_proj, value_mix, value_proj):
    win, comp = communicate(key_rows, values, key_mix, key_proj, value_mix, value_proj)
    return attend(queries, gate_logits, win.reshape(4, 576, 384), comp.reshape(4, 2048, 384))


def solution(mesh):
    rows = P(("ctx", "head"), None)
    return jax.shard_map(
        local, mesh=mesh, in_specs=(rows,) * 4 + (P(),) * 4, out_specs=rows, check_vma=False)
```

time: 379 us -> 124 us (0.33)
  the two profiles are of different devices: /device:TPU:1 before, /device:TPU:457 now
where the time goes in v1:
time: 124 us
  Pallas kernels  114 us (92%)
  local copies, waits for them, and re-layouts  10 us (8%)
    pallas_call x1, Pallas kernels, communicate(): pl.pallas_call(comm_kernel, out_shape=(jax.ShapeDtypeStruct((4, 9, 64, 38...  78.4 us
    pallas_call x1, Pallas kernels, attend(): pl.pallas_call(attend_kernel, grid=(4,), in_specs=[pl.BlockSpec((64, 3072...  35.6 us
    unnamed x18, local copies, waits for them, and re-layouts  10 us

profile of v1, /device:TPU:457, one launch (start us, length us, event | category | flops | bytes accessed | tf_op | source)
XLA Modules:
  0.0 124.0 jit_solution(9314087802466802538)
XLA Ops:
  0.0 0.0 copy-start.2
  0.0 1.0 copy-done.2
  1.0 0.0 copy-start.3
  1.0 0.9 copy-done.3
  1.9 0.0 copy-start.4
  1.9 0.9 copy-done.4
  2.8 0.0 copy-start.5
  2.8 0.8 copy-done.5
  3.6 0.0 copy-start.6
  3.6 0.8 copy-done.6
  4.5 0.0 copy-start.7
  4.5 0.8 copy-done.7
  5.2 78.4 %shard_map.82 = (bf16[4,9,64,384]{3,2,1,0:T(8,128)(2,1)S(1)}, bf16[4,16,4,2,16,384]{5,4,3,2,1,0:T(8,128)(2,1)S(1)}) custom-call(bf16[64,768]{1,0:T(8,128)(2,1)S(1)} %copy-done.4, bf16[64,512]{1,0:T(8,128)(2,1)S(1)} %copy-done.5, bf16[4,32,192]{2,1,0:T(8,128)(2,1)S(1)} %copy-done.6, bf16[4,192,192]{2,1,0:T(8,128)(2,1)S(1)} %copy-done.2, ...), custom_call_target="tpu_custom_call" | custom-call | flops 100000000 | bytes 10000000 | tf_op jit(solution)/shard_map/pallas_call | solution.py:250
  83.6 0.0 copy-start
  83.6 2.7 %copy-done = bf16[4,16,4,2,16,384]{5,4,3,2,1,0:T(8,128)(2,1)} copy-done((bf16[4,16,4,2,16,384]{5,4,3,2,1,0:T(8,128)(2,1)}, bf16[4,16,4,2,16,384]{5,4,3,2,1,0:T(8,128)(2,1)S(1)}, u32[]{:S(2)}) %copy-start) | copy-done | bytes 6291480
  86.3 0.0 copy-start.1
  86.3 1.4 %copy-done.1 = bf16[64,12288]{1,0:T(8,128)(2,1)S(1)} copy-done((bf16[64,12288]{1,0:T(8,128)(2,1)S(1)}, bf16[64,12288]{1,0:T(8,128)(2,1)}, u32[]{:S(2)}) %copy-start.1) | copy-done | bytes 1572888
  87.7 0.0 copy-start.8
  87.7 0.7 copy-done.8
  88.4 35.6 %shard_map.83 = bf16[64,8192]{1,0:T(8,128)(2,1)} custom-call(bf16[64,12288]{1,0:T(8,128)(2,1)S(1)} %copy-done.1, bf16[64,128]{1,0:T(8,128)(2,1)S(1)} %copy-done.8, bf16[4,576,384]{2,1,0:T(8,128)(2,1)S(1)} %bitcast.3, bf16[4,2048,384]{2,1,0:T(8,128)(2,1)} %bitcast.2), custom_call_target="tpu_custom_call" | custom-call | tf_op jit(solution)/shard_map/pallas_call | solution.py:364
Async XLA Ops:
  0.0 1.0 copy-start.2
  1.0 0.9 copy-start.3
  1.9 0.9 copy-start.4
  2.8 0.8 copy-start.5
  3.6 0.8 copy-start.6
  4.5 0.8 copy-start.7
  83.6 2.7 %copy-start = (bf16[4,16,4,2,16,384]{5,4,3,2,1,0:T(8,128)(2,1)}, bf16[4,16,4,2,16,384]{5,4,3,2,1,0:T(8,128)(2,1)S(1)}, u32[]{:S(2)}) copy-start(bf16[4,16,4,2,16,384]{5,4,3,2,1,0:T(8,128)(2,1)S(1)} %get-tuple-element.8) | copy-start | bytes 18874372
  86.3 1.4 %copy-start.1 = (bf16[64,12288]{1,0:T(8,128)(2,1)S(1)}, bf16[64,12288]{1,0:T(8,128)(2,1)}, u32[]{:S(2)}) copy-start(bf16[64,12288]{1,0:T(8,128)(2,1)} %q_ref.1) | copy-start | bytes 4718596
  87.7 0.7 copy-start.8

commit v2 on v0

v2 whole, which is shorter than its diff:
```python
import math

import jax
import jax.numpy as jnp
from jax import lax
from jax.experimental import pallas as pl
from jax.experimental.pallas import tpu as pltpu
from jax.sharding import PartitionSpec as P

BF = jnp.bfloat16
F32 = jnp.float32
MESH = pl.DeviceIdType.MESH
UNITS = 512
SCALE = 1.0 / math.sqrt(192.0)
NEG = -1e30
FLOOR = -1e29
RT = 512
KC = 1024
WK = 576


def loop(lower, upper, act):
    def body(i, carry):
        act(i)
        return carry

    lax.fori_loop(lower, upper, body, 0)


def fused_kernel(
    q_ref, kr, vr, gates, kmix, kproj, vmix, vproj,
    out,
    own, prev, mix, kp, quad, piece, win, comp, qs, gw, gc, vx, acc, mx, owin, s0, s1, bw, bc,
    prev_s, prev_r, win_s, win_r, own_sem, rel_s, rel_r, quad_s, quad_r, z_s, z_r,
    a_s, a_r, b_s, b_r, d_s, d_r,
):
    ctx = lax.axis_index("ctx")
    x = lax.axis_index("head")
    z = ctx // 8
    y = (ctx // 2) % 4
    c = ctx % 2
    row = ctx // 2
    unit = ctx * 4 + x
    par = x % 2
    half = x // 2
    member = 2 * c + par
    zp = (z + par + 1) % 2
    base = 8 * row + x - 8
    sibling = (ctx - c + (1 - c), x)

    def dev(v):
        return (v // 4, v % 4)

    def remote(src, dst, send, recv, device):
        return pltpu.make_async_remote_copy(
            src_ref=src, dst_ref=dst, send_sem=send, recv_sem=recv, device_id=device, device_id_type=MESH)

    barrier = pltpu.get_barrier_semaphore()

    def greet(device):
        pl.semaphore_signal(barrier, inc=1, device_id=device, device_id_type=MESH)

    def later(act):
        loop(0, (16 - z - par) // 2, lambda i: act(z + 2 * i + 2 - (1 - par)))

    def earlier(act):
        loop(0, (z + 1 - par) // 2, lambda i: act(z - 2 * i - 2 + (1 - par)))

    earlier(lambda zz: greet((zz * 8 + y * 2 + c, x)))

    @pl.when(unit > 0)
    def _():
        greet(dev(unit - 1))

    for m in range(1, 4):
        greet((ctx - c + (c + m // 2) % 2, x - par + (par + m % 2) % 2))
        greet((ctx, (x + m) % 4))
        greet((z * 8 + ((y + m) % 4) * 2 + c, x))
    greet(sibling)

    def source_slots(act):
        def one(s):
            @pl.when(jnp.logical_and(base + s >= 0, s != 8 + 4 * c))
            def _():
                act(s)

        loop(0, 13, one)

    source_slots(lambda s: greet(dev(base + s)))

    for h in range(2):
        own[h, :, 0:384] = kr[:, 384 * h:384 * h + 384]
        own[h, :, 384:640] = vr[:, 256 * h:256 * h + 256]
        mix[h, :, 0:192] = kmix[2 * h].astype(F32)
        mix[h, :, 192:384] = kmix[2 * h + 1].astype(F32)
        mix[h, :, 384:512] = vmix[2 * h].astype(F32)
        mix[h, :, 512:640] = vmix[2 * h + 1].astype(F32)
        kp[h] = jnp.zeros((384, 384), BF)
        kp[h, 0:192, 0:192] = kproj[2 * h]
        kp[h, 192:384, 192:384] = kproj[2 * h + 1]

    next_row = (row < 63).astype(jnp.int32)
    targets = jnp.where(c == 0, 7 + next_row * 2 * (x + 1), 2 * (3 - x) + 1 + next_row * 8)
    pl.semaphore_wait(
        barrier,
        targets + (unit < UNITS - 1).astype(jnp.int32) + 10 + (16 - z - par) // 2)

    def prev_copy(device):
        return remote(own.at[:, 48:64, :], prev, prev_s, prev_r, device)

    @pl.when(unit < UNITS - 1)
    def _():
        prev_copy(dev(unit + 1)).start()

    @pl.when(row == 0)
    def _():
        def clear(s):
            win[c, s] = jnp.zeros((64, 640), BF)

        loop(0, 8 - x, clear)

    def clear_plane(zz):
        @pl.when(zz % 2 == zp)
        def _():
            comp[c, zz // 2, zz % 2, y, half] = jnp.zeros((16, 640), BF)

    loop(z + 1, 4 * (z // 4) + 4, clear_plane)

    @pl.when((z // 4) % 2 == 0)
    def _():
        def clear(i):
            comp[:, 2 * (z // 4) + 2 + i] = jnp.zeros((2, 2, 4, 2, 16, 640), BF)

        loop(0, 2, clear)

    @pl.when(unit > 0)
    def _():
        prev_copy(dev(unit)).wait_recv()

    @pl.when(unit == 0)
    def _():
        prev[...] = jnp.zeros_like(prev)

    rows16 = lax.broadcasted_iota(jnp.int32, (16, 1), 0)
    mine = rows16 // 4 == member
    no_block = jnp.logical_and(unit == 0, rows16 == 0)
    for h in range(2):
        rows = jnp.concatenate([prev[h].astype(F32), own[h].astype(F32)], 0).reshape(5, 16, 640)
        pooled = jnp.sum(rows[0:4] * mix[h, 0:16][None], axis=1)
        pooled = pooled + jnp.sum(rows[1:5] * mix[h, 16:32][None], axis=1)
        pooled = jnp.concatenate([pooled] * 4, 0)
        pooled = jnp.where(mine, pooled, 0.0).astype(BF)
        keys = jnp.dot(pooled[:, 0:384], kp[h], preferred_element_type=F32)
        v0 = jnp.dot(pooled[:, 384:512], vproj[2 * h], preferred_element_type=F32)
        v1 = jnp.dot(pooled[:, 512:640], vproj[2 * h + 1], preferred_element_type=F32)
        keys = jnp.where(no_block, keys[1:2], keys)
        quad[0, h, :, 0:384] = keys.astype(BF)
        quad[0, h, :, 384:512] = jnp.where(no_block, 0.0, v0).astype(BF)
        quad[0, h, :, 512:640] = jnp.where(no_block, 0.0, v1).astype(BF)

    def quad_copy(m_to, m_from, device):
        return remote(
            quad.at[0, m_to // 2], quad.at[1 + m_from // 2, m_from % 2], quad_s.at[m_to], quad_r.at[m_from], device)

    for m in range(4):
        @pl.when(m != member)
        def _():
            quad_copy(m, member, (ctx - c + m // 2, x - par + m % 2)).start()
    for m in range(4):
        @pl.when(m != member)
        def _():
            quad_copy(m, m, (ctx, x)).wait_recv()
    total = quad[0, c].astype(F32)
    for m in range(4):
        total = total + jnp.where(m == member, 0.0, quad[1 + m // 2, m % 2].astype(F32))
    piece[...] = total.astype(BF)

    @pl.when(par == 1)
    def _():
        comp[c, z // 2, z % 2, y, half] = piece[...]

    def z_copy(z_from, z_to):
        ref = comp.at[c, z_from // 2, z_from % 2, y, half]
        return remote(piece, ref, z_s.at[z_to], z_r.at[z_from], (z_to * 8 + y * 2 + c, x))

    later(lambda zz: z_copy(z, zz).start())

    def win_copy(h, nxt, x_to, slot, device):
        return remote(own.at[h], win.at[h, slot], win_s.at[h, nxt, x_to], win_r.at[slot], device)

    def win_targets(act):
        for nxt in range(2):
            for m in range(4):
                x_to = (x + m) % 4
                slot = unit - (8 * (row + nxt) + x_to - 8)
                needed = jnp.logical_and(slot >= 0, slot <= 12)
                needed = jnp.logical_and(needed, row + nxt < 64)
                for h in range(2):
                    ctx_to = 2 * (row + nxt) + h
                    other = jnp.logical_or(ctx_to != ctx, x_to != x)

                    @pl.when(jnp.logical_and(needed, other))
                    def _():
                        act(win_copy(h, nxt, x_to, slot, (ctx_to, x_to)))

    win_targets(lambda copy: copy.start())
    own_copy = pltpu.make_async_copy(own.at[c], win.at[c, 8 + 4 * c], own_sem)
    own_copy.start()

    lane = lax.broadcasted_iota(jnp.int32, (64, 256), 1)
    zero = jnp.zeros((64, 256), F32)
    for head in range(64):
        g, hh = head // 16, head % 16
        at = 384 * (head // 2) + 128 * (head % 2)
        t = q_ref[:, at:at + 256].astype(F32)
        if head % 2 != g % 2:
            t = pltpu.roll(t, 192 if head % 2 else 64, 1)
        t = jnp.where(lane < 192 if g % 2 == 0 else lane >= 64, t, zero)
        qs[g, 64 * hh:64 * hh + 64, :] = t.astype(BF)
    sig = jax.nn.sigmoid(gates[...].astype(F32))
    for head in range(64):
        g, hh = head // 16, head % 16
        gc[g, 64 * hh:64 * hh + 64, :] = jnp.broadcast_to(sig[:, 2 * head:2 * head + 1], (64, 128))
        gw[g, 64 * hh:64 * hh + 64, :] = jnp.broadcast_to(sig[:, 2 * head + 1:2 * head + 2], (64, 128))
    vx[:, :, 128:256] = jnp.ones((4, KC, 128), BF)

    i = lax.broadcasted_iota(jnp.int32, (64, WK), 0)
    k = lax.broadcasted_iota(jnp.int32, (64, WK), 1)
    bw[...] = jnp.where((k > i) & (k <= i + 512) & (k + 64 * (unit - 8) >= 0), 0.0, NEG)
    last_chunk = z // 8
    i = lax.broadcasted_iota(jnp.int32, (64, KC), 0)
    k = lax.broadcasted_iota(jnp.int32, (64, KC), 1)
    r = k % 128
    m = (r % 16) // 4
    u = 8 * (4 * (8 * last_chunk + k // 128) + r // 32) + 4 * (m // 2) + 2 * ((r % 32) // 16) + m % 2
    b = 4 * u - 1 + r % 4
    bc[...] = jnp.where((16 * b + 31 <= 64 * unit + i) & (b >= 0), 0.0, NEG)

    earlier(lambda zz: z_copy(zz, z).wait_recv())

    def peer(along_x, d):
        if along_x:
            return (ctx, (x + d) % 4)
        return (z * 8 + ((y + d) % 4) * 2 + c, x)

    def a_copy(ci, d, xx, yy):
        pp = (z + xx % 2 + 1) % 2
        ref = comp.at[c, pl.ds(2 * ci, 2), pp, yy, xx // 2]
        return remote(ref, ref, a_s.at[ci, d - 1], a_r.at[ci, d - 1], peer(ci % 2 == 0, d))

    def b_copy(ci, d, xx, yy):
        if ci % 2 == 0:
            ref = comp.at[c, pl.ds(2 * ci, 2), :, yy]
        else:
            ref = comp.at[c, pl.ds(2 * ci, 2), (z + xx % 2 + 1) % 2, :, xx // 2]
        return remote(ref, ref, b_s.at[ci, d - 1], b_r.at[ci, d - 1], peer(ci % 2 == 1, d))

    def d_copy(ci, cc):
        ref = comp.at[cc, pl.ds(2 * ci, 2)]
        return remote(ref, ref, d_s.at[ci], d_r.at[ci], sibling)

    def back(along_x, d):
        return ((x + 4 - d) % 4, y) if along_x else (x, (y + 4 - d) % 4)

    def chunks(which, act):
        for ci in which:
            @pl.when(4 * ci <= z)
            def _():
                act(ci)

    def send_a(ci):
        for d in (1, 3, 2):
            a_copy(ci, d, x, y).start()

    def send_b(ci):
        for d in (1, 3, 2):
            a_copy(ci, d, *back(ci % 2 == 0, d)).wait_recv()
        for d in (1, 3, 2):
            b_copy(ci, d, x, y).start()

    def send_d(ci):
        for d in (1, 3, 2):
            b_copy(ci, d, *back(ci % 2 == 1, d)).wait_recv()
        d_copy(ci, c).start()

    chunks((3, 2, 1, 0), send_a)

    def win_wait(s):
        remote(own.at[0], win.at[c, s], win_s.at[0, 0, 0], win_r.at[s], sibling).wait_recv()

    source_slots(win_wait)
    own_copy.wait()

    def relay(cc, first):
        ref = win.at[cc, pl.ds(4 * first, 9)]
        return remote(ref, ref, rel_s, rel_r, sibling)

    relay(c, 1 - c).start()
    relay(1 - c, c).wait_recv()

    def scores(g, tile, keys):
        q = qs[g, pl.ds(pl.multiple_of(tile * RT, RT), RT), :]
        return lax.dot_general(q, keys, (((1,), (1,)), ((), ())), preferred_element_type=F32)

    def biased(s, bias):
        width = s.shape[1]
        return (s.reshape(RT // 64, 64, width) + bias[...][None]).reshape(RT, width)

    def win_keys(h, odd):
        return win[h, pl.ds(4 * c, 9), :, 128 * odd:128 * odd + 256].reshape(WK, 256)

    def win_done(s, g, tile):
        rows = pl.ds(pl.multiple_of(tile * RT, RT), RT)
        s = biased(s, bw)
        top = jnp.max(s, axis=1, keepdims=True)
        p = jnp.exp((s - top) * SCALE).astype(BF)
        a = jnp.dot(p, vx[g, 0:WK, :], preferred_element_type=F32)
        owin[g, rows, :] = gw[g, rows, :] * a[:, 0:128] / a[:, 128:256]

    def comp_keys(h, odd, chunk):
        return comp[h, pl.ds(4 * chunk, 4), :, :, :, :, 128 * odd:128 * odd + 256].reshape(KC, 256)

    def comp_done(s, g, tile, first):
        rows = pl.ds(pl.multiple_of(tile * RT, RT), RT)
        if first:
            s = biased(s, bc)
            top = jnp.maximum(jnp.max(s, axis=1, keepdims=True), FLOOR)
            p = jnp.exp((s - top) * SCALE).astype(BF)
            acc[g, rows, :] = jnp.dot(p, vx[g], preferred_element_type=F32)
        else:
            before = mx[g, rows, 0:1]
            top = jnp.maximum(jnp.max(s, axis=1, keepdims=True), before)
            p = jnp.exp((s - top) * SCALE).astype(BF)
            factor = jnp.exp((before - top) * SCALE)
            acc[g, rows, :] = acc[g, rows, :] * factor + jnp.dot(p, vx[g], preferred_element_type=F32)
        mx[g, rows, :] = jnp.broadcast_to(top, (RT, 128))

    tiles = 1024 // RT

    def run_half(h, width, keys, done):
        s0[:, 0:width] = scores(2 * h, 0, keys(h, 0))

        def body(t):
            s1[:, 0:width] = scores(2 * h + 1, t, keys(h, 1))
            done(s0[:, 0:width], 2 * h, t)
            s0[:, 0:width] = scores(2 * h, jnp.minimum(t + 1, tiles - 1), keys(h, 0))
            done(s1[:, 0:width], 2 * h + 1, t)

        loop(0, tiles, body)

    for g in range(4):
        vx[g, 0:WK, 0:128] = win[
            g // 2, pl.ds(4 * c, 9), :, 384 + 128 * (g % 2):512 + 128 * (g % 2)].reshape(WK, 128)
    run_half(0, WK, win_keys, win_done)
    chunks((3, 2, 1, 0), send_b)
    run_half(1, WK, win_keys, win_done)

    def load_values(chunk):
        for g in range(4):
            at = 384 + 128 * (g % 2)
            vx[g, :, 0:128] = comp[g // 2, pl.ds(4 * chunk, 4), :, :, :, :, at:at + 128].reshape(KC, 128)
        weight = jnp.where(jnp.logical_and(chunk == 0, rows16 == 0), 0.0, 1.0).astype(BF)
        for g in range(4):
            vx[g, 0:16, 128:256] = jnp.broadcast_to(weight, (16, 128))

    def ready(which):
        chunks(which, send_d)
        chunks(which, lambda ci: d_copy(ci, 1 - c).wait_recv())

    @pl.when(z >= 8)
    def _():
        ready((3, 2))

    @pl.when(z < 8)
    def _():
        ready((1, 0))

    load_values(last_chunk)

    def first_pass(h):
        run_half(h, KC, lambda hh, odd: comp_keys(hh, odd, last_chunk),
                 lambda s, g, t: comp_done(s, g, t, True))

    loop(0, 2, first_pass)

    @pl.when(z >= 8)
    def _():
        ready((1, 0))
        load_values(jnp.int32(0))
        loop(0, 2, lambda h: run_half(
            h, KC, lambda hh, odd: comp_keys(hh, odd, 0), lambda s, g, t: comp_done(s, g, t, False)))

    for g in range(4):
        for hh in range(16):
            rows = slice(64 * hh, 64 * hh + 64)
            weight = acc[g, rows, 128:256]
            o = gc[g, rows, :] * acc[g, rows, 0:128] / jnp.where(weight > 0.0, weight, 1.0) + owin[g, rows, :]
            at = 128 * (16 * g + hh)
            out[:, at:at + 128] = o.astype(BF)

    def sent(ci):
        d_copy(ci, c).wait_send()
        for d in (1, 2, 3):
            a_copy(ci, d, x, y).wait_send()
            b_copy(ci, d, x, y).wait_send()

    chunks((3, 2, 1, 0), sent)
    relay(c, 1 - c).wait_send()
    win_targets(lambda copy: copy.wait_send())
    later(lambda zz: z_copy(z, zz).wait_send())
    for m in range(4):
        @pl.when(m != member)
        def _():
            quad_copy(m, member, (ctx, x)).wait_send()

    @pl.when(unit < UNITS - 1)
    def _():
        prev_copy(dev(unit)).wait_send()


def local(queries, key_rows, values, gate_logits, key_mix, key_proj, value_mix, value_proj):
    dma = pltpu.SemaphoreType.DMA
    vmem = pl.BlockSpec(memory_space=pltpu.VMEM)
    return pl.pallas_call(
        fused_kernel,
        out_shape=jax.ShapeDtypeStruct((64, 8192), BF),
        in_specs=[vmem] * 8,
        out_specs=vmem,
        scratch_shapes=[
            pltpu.VMEM((2, 64, 640), BF),
            pltpu.VMEM((2, 16, 640), BF),
            pltpu.VMEM((2, 32, 640), F32),
            pltpu.VMEM((2, 384, 384), BF),
            pltpu.VMEM((3, 2, 16, 640), BF),
            pltpu.VMEM((16, 640), BF),
            pltpu.VMEM((2, 13, 64, 640), BF),
            pltpu.VMEM((2, 8, 2, 4, 2, 16, 640), BF),
            pltpu.VMEM((4, 1024, 256), BF),
            pltpu.VMEM((4, 1024, 128), F32),
            pltpu.VMEM((4, 1024, 128), F32),
            pltpu.VMEM((4, KC, 256), BF),
            pltpu.VMEM((4, 1024, 256), F32),
            pltpu.VMEM((4, 1024, 128), F32),
            pltpu.VMEM((4, 1024, 128), F32),
            pltpu.VMEM((RT, KC), F32),
            pltpu.VMEM((RT, KC), F32),
            pltpu.VMEM((64, WK), F32),
            pltpu.VMEM((64, KC), F32),
            dma, dma, dma((2, 2, 4)), dma((13,)), dma, dma, dma, dma((4,)), dma((4,)), dma((16,)), dma((16,)),
            dma((4, 3)), dma((4, 3)), dma((4, 3)), dma((4, 3)), dma((4,)), dma((4,)),
        ],
        compiler_params=pltpu.CompilerParams(
            collective_id=0, has_side_effects=True, vmem_limit_bytes=56 * 2**20),
        cost_estimate=pl.CostEstimate(flops=10**10, bytes_accessed=10**7, transcendentals=10**7),
    )(queries, key_rows, values, gate_logits, key_mix, key_proj, value_mix, value_proj)


def solution(mesh):
    rows = P(("ctx", "head"), None)
    return jax.shard_map(
        local, mesh=mesh, in_specs=(rows,) * 4 + (P(),) * 4, out_specs=rows, check_vma=False)
```

time: 379 us -> 82.1 us (0.22)
  the two profiles are of different devices: /device:TPU:1 before, /device:TPU:272 now
where the time goes in v2:
time: 82.1 us; the launch traced here: 81.9 us
  Pallas kernels  79.7 us (97%)
  local copies, waits for them, and re-layouts  2.26 us (3%)
    pallas_call x1, Pallas kernels, local(): pl.pallas_call(fused_kernel, out_shape=jax.ShapeDtypeStruct((64, 8192), B...  79.7 us
    unnamed x1, local copies, waits for them, and re-layouts  2.26 us

profile of v2, /device:TPU:272, one launch (start us, length us, event | category | flops | bytes accessed | tf_op | source)
XLA Modules:
  0.0 81.9 jit_solution(4445365816535925736)
XLA Ops:
  0.0 79.7 %shard_map.82 = bf16[64,8192]{1,0:T(8,128)(2,1)} custom-call(bf16[64,12288]{1,0:T(8,128)(2,1)} %q_ref.1, bf16[64,768]{1,0:T(8,128)(2,1)} %kr.1, bf16[64,512]{1,0:T(8,128)(2,1)} %vr.1, bf16[64,128]{1,0:T(8,128)(2,1)} %gates.1, bf16[4,32,192]{2,1,0:T(8,128)(2,1)} %kmix.1, bf16[4,192,192]{2,1,0:T(8,128)(2,1)} %kproj.1, bf16[4,32,128]{2,1,0:T(8,128)(2,1)} %vmix.1, ...), custom_call_target="tpu_custom_call" | custom-call | flops 10000000000 | bytes 10000000 | tf_op jit(solution)/shard_map/pallas_call | solution.py:424
  79.7 2.3 %copy.10 = bf16[64,8192]{1,0:T(8,128)(2,1)} copy(bf16[64,8192]{1,0:T(8,128)(2,1)} %shard_map.82) | data formatting | bytes 2097152

commit v3 on v2

--- a/solution.py
+++ b/solution.py
@@ -28,12 +28,14 @@
 
 
 def fused_kernel(
-    q_ref, kr, vr, gates, kmix, kproj, vmix, vproj,
+    q_any, kr, vr, gates, kmix, kproj, vmix, vproj,
     out,
-    own, prev, mix, kp, quad, piece, win, comp, qs, gw, gc, vx, acc, mx, owin, s0, s1, bw, bc,
-    prev_s, prev_r, win_s, win_r, own_sem, rel_s, rel_r, quad_s, quad_r, z_s, z_r,
+    q_ref, own, prev, mix, kp, quad, piece, win, comp, qs, gw, gc, vx, acc, mx, owin, s0, s1, bw, bc,
+    q_sem, prev_s, prev_r, win_s, win_r, own_sem, rel_s, rel_r, quad_s, quad_r, z_s, z_r,
     a_s, a_r, b_s, b_r, d_s, d_r,
 ):
+    q_copy = pltpu.make_async_copy(q_any, q_ref, q_sem)
+    q_copy.start()
     ctx = lax.axis_index("ctx")
     x = lax.axis_index("head")
     z = ctx // 8
@@ -111,6 +113,28 @@
     @pl.when(unit < UNITS - 1)
     def _():
         prev_copy(dev(unit + 1)).start()
+
+    def win_copy(h, nxt, x_to, slot, device):
+        return remote(own.at[h], win.at[h, slot], win_s.at[h, nxt, x_to], win_r.at[slot], device)
+
+    def win_targets(act):
+        for nxt in range(2):
+            for m in range(4):
+                x_to = (x + m) % 4
+                slot = unit - (8 * (row + nxt) + x_to - 8)
+                needed = jnp.logical_and(slot >= 0, slot <= 12)
+                needed = jnp.logical_and(needed, row + nxt < 64)
+                for h in range(2):
+                    ctx_to = 2 * (row + nxt) + h
+                    other = jnp.logical_or(ctx_to != ctx, x_to != x)
+
+                    @pl.when(jnp.logical_and(needed, other))
+                    def _():
+                        act(win_copy(h, nxt, x_to, slot, (ctx_to, x_to)))
+
+    win_targets(lambda copy: copy.start())
+    own_copy = pltpu.make_async_copy(own.at[c], win.at[c, 8 + 4 * c], own_sem)
+    own_copy.start()
 
     @pl.when(row == 0)
     def _():
@@ -185,30 +209,9 @@
 
     later(lambda zz: z_copy(z, zz).start())
 
-    def win_copy(h, nxt, x_to, slot, device):
-        return remote(own.at[h], win.at[h, slot], win_s.at[h, nxt, x_to], win_r.at[slot], device)
-
-    def win_targets(act):
-        for nxt in range(2):
-            for m in range(4):
-                x_to = (x + m) % 4
-                slot = unit - (8 * (row + nxt) + x_to - 8)
-                needed = jnp.logical_and(slot >= 0, slot <= 12)
-                needed = jnp.logical_and(needed, row + nxt < 64)
-                for h in range(2):
-                    ctx_to = 2 * (row + nxt) + h
-                    other = jnp.logical_or(ctx_to != ctx, x_to != x)
-
-                    @pl.when(jnp.logical_and(needed, other))
-                    def _():
-                        act(win_copy(h, nxt, x_to, slot, (ctx_to, x_to)))
-
-    win_targets(lambda copy: copy.start())
-    own_copy = pltpu.make_async_copy(own.at[c], win.at[c, 8 + 4 * c], own_sem)
-    own_copy.start()
-
     lane = lax.broadcasted_iota(jnp.int32, (64, 256), 1)
     zero = jnp.zeros((64, 256), F32)
+    q_copy.wait()
     for head in range(64):
         g, hh = head // 16, head % 16
         at = 384 * (head // 2) + 128 * (head % 2)
@@ -296,7 +299,6 @@
         return remote(ref, ref, rel_s, rel_r, sibling)
 
     relay(c, 1 - c).start()
-    relay(1 - c, c).wait_recv()
 
     def scores(g, tile, keys):
         q = qs[g, pl.ds(pl.multiple_of(tile * RT, RT), RT), :]
@@ -348,47 +350,59 @@
 
         loop(0, tiles, body)
 
-    for g in range(4):
-        vx[g, 0:WK, 0:128] = win[
-            g // 2, pl.ds(4 * c, 9), :, 384 + 128 * (g % 2):512 + 128 * (g % 2)].reshape(WK, 128)
-    run_half(0, WK, win_keys, win_done)
-    chunks((3, 2, 1, 0), send_b)
-    run_half(1, WK, win_keys, win_done)
-
-    def load_values(chunk):
-        for g in range(4):
-            at = 384 + 128 * (g % 2)
-            vx[g, :, 0:128] = comp[g // 2, pl.ds(4 * chunk, 4), :, :, :, :, at:at + 128].reshape(KC, 128)
+    def win_half(h):
+        for odd in range(2):
+            at = 384 + 128 * odd
+            vx[2 * h + odd, 0:WK, 0:128] = win[h, pl.ds(4 * c, 9), :, at:at + 128].reshape(WK, 128)
+        run_half(h, WK, win_keys, win_done)
+
+    def comp_half(h, chunk, first):
+        for odd in range(2):
+            at = 384 + 128 * odd
+            vx[2 * h + odd, :, 0:128] = comp[h, pl.ds(4 * chunk, 4), :, :, :, :, at:at + 128].reshape(KC, 128)
         weight = jnp.where(jnp.logical_and(chunk == 0, rows16 == 0), 0.0, 1.0).astype(BF)
-        for g in range(4):
-            vx[g, 0:16, 128:256] = jnp.broadcast_to(weight, (16, 128))
-
-    def ready(which):
-        chunks(which, send_d)
-        chunks(which, lambda ci: d_copy(ci, 1 - c).wait_recv())
+        for odd in range(2):
+            vx[2 * h + odd, 0:16, 128:256] = jnp.broadcast_to(weight, (16, 128))
+        run_half(h, KC, lambda hh, odd: comp_keys(hh, odd, chunk),
+                 lambda s, g, t: comp_done(s, g, t, first))
+
+    def nearest(act):
+        @pl.when(z >= 8)
+        def _():
+            chunks((3, 2), act)
+
+        @pl.when(z < 8)
+        def _():
+            chunks((1, 0), act)
+
+    def farther(act):
+        @pl.when(z >= 8)
+        def _():
+            chunks((1, 0), act)
+
+    def wait_d(ci):
+        d_copy(ci, 1 - c).wait_recv()
+
+    win_half(c)
+    nearest(send_b)
+    relay(1 - c, c).wait_recv()
+    win_half(1 - c)
+    nearest(send_d)
+    farther(send_b)
+    comp_half(c, last_chunk, True)
+    nearest(wait_d)
+    comp_half(1 - c, last_chunk, True)
+    farther(send_d)
 
     @pl.when(z >= 8)
     def _():
-        ready((3, 2))
-
-    @pl.when(z < 8)
-    def _():
-        ready((1, 0))
-
-    load_values(last_chunk)
-
-    def first_pass(h):
-        run_half(h, KC, lambda hh, odd: comp_keys(hh, odd, last_chunk),
-                 lambda s, g, t: comp_done(s, g, t, True))
-
-    loop(0, 2, first_pass)
+        comp_half(c, jnp.int32(0), False)
+
+    farther(wait_d)
 
     @pl.when(z >= 8)
     def _():
-        ready((1, 0))
-        load_values(jnp.int32(0))
-        loop(0, 2, lambda h: run_half(
-            h, KC, lambda hh, odd: comp_keys(hh, odd, 0), lambda s, g, t: comp_done(s, g, t, False)))
+        comp_half(1 - c, jnp.int32(0), False)
 
     for g in range(4):
         for hh in range(16):
@@ -424,9 +438,10 @@
     return pl.pallas_call(
         fused_kernel,
         out_shape=jax.ShapeDtypeStruct((64, 8192), BF),
-        in_specs=[vmem] * 8,
+        in_specs=[pl.BlockSpec(memory_space=pl.ANY)] + [vmem] * 7,
         out_specs=vmem,
         scratch_shapes=[
+            pltpu.VMEM((64, 12288), BF),
             pltpu.VMEM((2, 64, 640), BF),
             pltpu.VMEM((2, 16, 640), BF),
             pltpu.VMEM((2, 32, 640), F32),
@@ -446,7 +461,7 @@
             pltpu.VMEM((RT, KC), F32),
             pltpu.VMEM((64, WK), F32),
             pltpu.VMEM((64, KC), F32),
-            dma, dma, dma((2, 2, 4)), dma((13,)), dma, dma, dma, dma((4,)), dma((4,)), dma((16,)), dma((16,)),
+            dma, dma, dma, dma((2, 2, 4)), dma((13,)), dma, dma, dma, dma((4,)), dma((4,)), dma((16,)), dma((16,)),
             dma((4, 3)), dma((4, 3)), dma((4, 3)), dma((4, 3)), dma((4,)), dma((4,)),
         ],
         compiler_params=pltpu.CompilerParams(

time: 82.1 us -> 73.4 us (0.89)
  the two profiles are of different devices: /device:TPU:272 before, /device:TPU:288 now
where the time goes in v3:
time: 73.4 us; the launch traced here: 73.3 us
  Pallas kernels  71 us (97%)
  local copies, waits for them, and re-layouts  2.26 us (3%)
    pallas_call x1, Pallas kernels, local(): pl.pallas_call(fused_kernel, out_shape=jax.ShapeDtypeStruct((64, 8192), B...  71 us
    unnamed x1, local copies, waits for them, and re-layouts  2.26 us

profile of v3, /device:TPU:288, one launch (start us, length us, event | category | flops | bytes accessed | tf_op | source)
XLA Modules:
  0.0 73.3 jit_solution(15376373609823225015)
XLA Ops:
  0.0 71.0 %shard_map.82 = bf16[64,8192]{1,0:T(8,128)(2,1)} custom-call(bf16[64,12288]{1,0:T(8,128)(2,1)} %q_any.1, bf16[64,768]{1,0:T(8,128)(2,1)} %kr.1, bf16[64,512]{1,0:T(8,128)(2,1)} %vr.1, bf16[64,128]{1,0:T(8,128)(2,1)} %gates.1, bf16[4,32,192]{2,1,0:T(8,128)(2,1)} %kmix.1, bf16[4,192,192]{2,1,0:T(8,128)(2,1)} %kproj.1, bf16[4,32,128]{2,1,0:T(8,128)(2,1)} %vmix.1, ...), custom_call_target="tpu_custom_call" | custom-call | flops 10000000000 | bytes 10000000 | tf_op jit(solution)/shard_map/pallas_call | solution.py:438
  71.0 2.3 %copy.10 = bf16[64,8192]{1,0:T(8,128)(2,1)} copy(bf16[64,8192]{1,0:T(8,128)(2,1)} %shard_map.82) | data formatting | bytes 2097152

commit v4 on v3

--- a/solution.py
+++ b/solution.py
@@ -30,9 +30,9 @@
 def fused_kernel(
     q_any, kr, vr, gates, kmix, kproj, vmix, vproj,
     out,
-    q_ref, own, prev, mix, kp, quad, piece, win, comp, qs, gw, gc, vx, acc, mx, owin, s0, s1, bw, bc,
-    q_sem, prev_s, prev_r, win_s, win_r, own_sem, rel_s, rel_r, quad_s, quad_r, z_s, z_r,
-    a_s, a_r, b_s, b_r, d_s, d_r,
+    q_ref, own, mix, kp, tile, tail, quad, tail_in, piece, win, comp, qs, gw, gc, vx, acc, mx, owin, s0, s1, bw, bc,
+    q_sem, tail_s, tail_r, win_s, win_r, own_sem, rel_s, rel_r, quad_s, quad_r, z_s, z_r,
+    a_s, a_r, b_s, b_r, d_s, d_r, pass_s,
 ):
     q_copy = pltpu.make_async_copy(q_any, q_ref, q_sem)
     q_copy.start()
@@ -70,9 +70,13 @@
 
     earlier(lambda zz: greet((zz * 8 + y * 2 + c, x)))
 
-    @pl.when(unit > 0)
-    def _():
-        greet(dev(unit - 1))
+    def run_before(k):
+        return 8 * row + 4 * k + 2 * half - 1
+
+    for k in range(2):
+        @pl.when(run_before(k) >= 0)
+        def _():
+            greet(dev(run_before(k)))
 
     for m in range(1, 4):
         greet((ctx - c + (c + m // 2) % 2, x - par + (par + m % 2) % 2))
@@ -88,7 +92,12 @@
 
         loop(0, 13, one)
 
-    source_slots(lambda s: greet(dev(base + s)))
+    def greet_source(s):
+        v = base + s
+        passed = jnp.logical_and(v < 8 * row, v % 4 != x)
+        greet((jnp.where(passed, ctx, v // 4), v % 4))
+
+    source_slots(greet_source)
 
     for h in range(2):
         own[h, :, 0:384] = kr[:, 384 * h:384 * h + 384]
@@ -101,25 +110,54 @@
         kp[h, 0:192, 0:192] = kproj[2 * h]
         kp[h, 192:384, 192:384] = kproj[2 * h + 1]
 
+    rows16 = lax.broadcasted_iota(jnp.int32, (16, 1), 0)
+    crosses = jnp.logical_and(par == 1, unit < UNITS - 1)
+    for h in range(2):
+        rows = own[h].astype(F32).reshape(4, 16, 640)
+        begins = jnp.sum(rows * mix[h, 0:16][None], axis=1)
+        ends = jnp.sum(rows * mix[h, 16:32][None], axis=1)
+        shares = jnp.concatenate([ends[0:1], ends[1:4] + begins[0:3]], 0)
+        placed = jnp.where(rows16 // 4 == member, jnp.concatenate([shares] * 4, 0), 0.0)
+        within = jnp.logical_and(rows16 == 4 * (member + 1), par == 0)
+        tile[h] = placed + jnp.where(within, begins[3:4], 0.0)
+        tail[h] = jnp.where(rows16[0:8] == 0, begins[3:4], 0.0)
+
     next_row = (row < 63).astype(jnp.int32)
-    targets = jnp.where(c == 0, 7 + next_row * 2 * (x + 1), 2 * (3 - x) + 1 + next_row * 8)
+    targets = jnp.where(c == 0, 7, 2 * (3 - x) + 1) + 2 * next_row + jnp.where(row > 0, x + 3, 0)
     pl.semaphore_wait(
         barrier,
-        targets + (unit < UNITS - 1).astype(jnp.int32) + 10 + (16 - z - par) // 2)
-
-    def prev_copy(device):
-        return remote(own.at[:, 48:64, :], prev, prev_s, prev_r, device)
-
-    @pl.when(unit < UNITS - 1)
-    def _():
-        prev_copy(dev(unit + 1)).start()
+        targets + 4 * crosses.astype(jnp.int32) + 10 + (16 - z - par) // 2)
+
+    def quad_copy(m_to, m_from, device):
+        return remote(tile.at[m_to // 2], quad.at[m_from], quad_s.at[m_to], quad_r.at[m_from], device)
+
+    for m in range(4):
+        @pl.when(m != member)
+        def _():
+            quad_copy(m, member, (ctx - c + m // 2, x - par + m % 2)).start()
+
+    follower = unit + 1
+    run = (follower % 8) // 4
+
+    def tail_copy(h, p):
+        device = (2 * (follower // 8) + h, 2 * ((follower % 4) // 2) + p)
+        return remote(tail.at[h], tail_in.at[run], tail_s.at[h, p], tail_r.at[run], device)
+
+    def tails(act):
+        @pl.when(crosses)
+        def _():
+            for h in range(2):
+                for p in range(2):
+                    act(tail_copy(h, p))
+
+    tails(lambda copy: copy.start())
 
     def win_copy(h, nxt, x_to, slot, device):
         return remote(own.at[h], win.at[h, slot], win_s.at[h, nxt, x_to], win_r.at[slot], device)
 
     def win_targets(act):
         for nxt in range(2):
-            for m in range(4):
+            for m in range(4 - 3 * nxt):
                 x_to = (x + m) % 4
                 slot = unit - (8 * (row + nxt) + x_to - 8)
                 needed = jnp.logical_and(slot >= 0, slot <= 12)
@@ -157,47 +195,31 @@
 
         loop(0, 2, clear)
 
-    @pl.when(unit > 0)
-    def _():
-        prev_copy(dev(unit)).wait_recv()
-
-    @pl.when(unit == 0)
-    def _():
-        prev[...] = jnp.zeros_like(prev)
-
-    rows16 = lax.broadcasted_iota(jnp.int32, (16, 1), 0)
-    mine = rows16 // 4 == member
-    no_block = jnp.logical_and(unit == 0, rows16 == 0)
-    for h in range(2):
-        rows = jnp.concatenate([prev[h].astype(F32), own[h].astype(F32)], 0).reshape(5, 16, 640)
-        pooled = jnp.sum(rows[0:4] * mix[h, 0:16][None], axis=1)
-        pooled = pooled + jnp.sum(rows[1:5] * mix[h, 16:32][None], axis=1)
-        pooled = jnp.concatenate([pooled] * 4, 0)
-        pooled = jnp.where(mine, pooled, 0.0).astype(BF)
-        keys = jnp.dot(pooled[:, 0:384], kp[h], preferred_element_type=F32)
-        v0 = jnp.dot(pooled[:, 384:512], vproj[2 * h], preferred_element_type=F32)
-        v1 = jnp.dot(pooled[:, 512:640], vproj[2 * h + 1], preferred_element_type=F32)
-        keys = jnp.where(no_block, keys[1:2], keys)
-        quad[0, h, :, 0:384] = keys.astype(BF)
-        quad[0, h, :, 384:512] = jnp.where(no_block, 0.0, v0).astype(BF)
-        quad[0, h, :, 512:640] = jnp.where(no_block, 0.0, v1).astype(BF)
-
-    def quad_copy(m_to, m_from, device):
-        return remote(
-            quad.at[0, m_to // 2], quad.at[1 + m_from // 2, m_from % 2], quad_s.at[m_to], quad_r.at[m_from], device)
-
+    total = tile[c]
     for m in range(4):
         @pl.when(m != member)
         def _():
-            quad_copy(m, member, (ctx - c + m // 2, x - par + m % 2)).start()
+            quad_copy(m, m, (ctx, x)).wait_recv()
+    for k in range(2):
+        @pl.when(run_before(k) >= 0)
+        def _():
+            remote(tail.at[0], tail_in.at[k], tail_s.at[0, 0], tail_r.at[k], sibling).wait_recv()
+
+        @pl.when(run_before(k) < 0)
+        def _():
+            tail_in[k] = jnp.zeros((8, 640), F32)
+
     for m in range(4):
-        @pl.when(m != member)
-        def _():
-            quad_copy(m, m, (ctx, x)).wait_recv()
-    total = quad[0, c].astype(F32)
-    for m in range(4):
-        total = total + jnp.where(m == member, 0.0, quad[1 + m // 2, m % 2].astype(F32))
-    piece[...] = total.astype(BF)
+        total = total + jnp.where(m == member, 0.0, quad[m])
+    total = total + jnp.concatenate([tail_in[0], tail_in[1]], 0)
+    pooled = total.astype(BF)
+    keys = jnp.dot(pooled[:, 0:384], kp[c], preferred_element_type=F32)
+    v0 = jnp.dot(pooled[:, 384:512], vproj[2 * c], preferred_element_type=F32)
+    v1 = jnp.dot(pooled[:, 512:640], vproj[2 * c + 1], preferred_element_type=F32)
+    no_block = jnp.logical_and(jnp.logical_and(row == 0, half == 0), rows16 == 0)
+    piece[:, 0:384] = jnp.where(no_block, keys[1:2], keys).astype(BF)
+    piece[:, 384:512] = jnp.where(no_block, 0.0, v0).astype(BF)
+    piece[:, 512:640] = jnp.where(no_block, 0.0, v1).astype(BF)
 
     @pl.when(par == 1)
     def _():
@@ -239,6 +261,26 @@
     b = 4 * u - 1 + r % 4
     bc[...] = jnp.where((16 * b + 31 <= 64 * unit + i) & (b >= 0), 0.0, NEG)
 
+    def pass_copy(k, m):
+        x_to = (x + m) % 4
+        return remote(
+            win.at[c, 4 * k], win.at[c, 4 * k + x - x_to], pass_s.at[k, m], win_r.at[4 * k + x - x_to], (ctx, x_to))
+
+    def passes(k, act):
+        for m in (1, 3, 2):
+            @pl.when(jnp.logical_or(k == 1, (x + m) % 4 < x))
+            def _():
+                act(pass_copy(k, m))
+
+    def win_wait(s):
+        remote(own.at[0], win.at[c, s], win_s.at[0, 0, 0], win_r.at[s], sibling).wait_recv()
+
+    @pl.when(row > 0)
+    def _():
+        for k in (1, 0):
+            win_wait(4 * k)
+            passes(k, lambda copy: copy.start())
+
     earlier(lambda zz: z_copy(zz, z).wait_recv())
 
     def peer(along_x, d):
@@ -288,10 +330,12 @@
 
     chunks((3, 2, 1, 0), send_a)
 
-    def win_wait(s):
-        remote(own.at[0], win.at[c, s], win_s.at[0, 0, 0], win_r.at[s], sibling).wait_recv()
-
-    source_slots(win_wait)
+    def win_rest(s):
+        @pl.when(jnp.logical_and(s != 0, s != 4))
+        def _():
+            win_wait(s)
+
+    source_slots(win_rest)
     own_copy.wait()
 
     def relay(cc, first):
@@ -421,15 +465,19 @@
     chunks((3, 2, 1, 0), sent)
     relay(c, 1 - c).wait_send()
     win_targets(lambda copy: copy.wait_send())
+
+    @pl.when(row > 0)
+    def _():
+        for k in (1, 0):
+            passes(k, lambda copy: copy.wait_send())
+
     later(lambda zz: z_copy(z, zz).wait_send())
     for m in range(4):
         @pl.when(m != member)
         def _():
             quad_copy(m, member, (ctx, x)).wait_send()
 
-    @pl.when(unit < UNITS - 1)
-    def _():
-        prev_copy(dev(unit)).wait_send()
+    tails(lambda copy: copy.wait_send())
 
 
 def local(queries, key_rows, values, gate_logits, key_mix, key_proj, value_mix, value_proj):
@@ -443,10 +491,12 @@
         scratch_shapes=[
             pltpu.VMEM((64, 12288), BF),
             pltpu.VMEM((2, 64, 640), BF),
-            pltpu.VMEM((2, 16, 640), BF),
             pltpu.VMEM((2, 32, 640), F32),
             pltpu.VMEM((2, 384, 384), BF),
-            pltpu.VMEM((3, 2, 16, 640), BF),
+            pltpu.VMEM((2, 16, 640), F32),
+            pltpu.VMEM((2, 8, 640), F32),
+            pltpu.VMEM((4, 16, 640), F32),
+            pltpu.VMEM((2, 8, 640), F32),
             pltpu.VMEM((16, 640), BF),
             pltpu.VMEM((2, 13, 64, 640), BF),
             pltpu.VMEM((2, 8, 2, 4, 2, 16, 640), BF),
@@ -461,8 +511,8 @@
             pltpu.VMEM((RT, KC), F32),
             pltpu.VMEM((64, WK), F32),
             pltpu.VMEM((64, KC), F32),
-            dma, dma, dma, dma((2, 2, 4)), dma((13,)), dma, dma, dma, dma((4,)), dma((4,)), dma((16,)), dma((16,)),
-            dma((4, 3)), dma((4, 3)), dma((4, 3)), dma((4, 3)), dma((4,)), dma((4,)),
+            dma, dma((2, 2)), dma((2,)), dma((2, 2, 4)), dma((13,)), dma, dma, dma, dma((4,)), dma((4,)), dma((16,)), dma((16,)),
+            dma((4, 3)), dma((4, 3)), dma((4, 3)), dma((4, 3)), dma((4,)), dma((4,)), dma((2, 4)),
         ],
         compiler_params=pltpu.CompilerParams(
             collective_id=0, has_side_effects=True, vmem_limit_bytes=56 * 2**20),

time: 73.4 us -> 63.6 us (0.87)
  the two profiles are of different devices: /device:TPU:288 before, /device:TPU:1 now
where the time goes in v4:
time: 63.6 us; the launch traced here: 62.4 us
  Pallas kernels  60.1 us (94%)
  local copies, waits for them, and re-layouts  2.26 us (4%)
    pallas_call x1, Pallas kernels, local(): pl.pallas_call(fused_kernel, out_shape=jax.ShapeDtypeStruct((64, 8192), B...  60.1 us
    unnamed x1, local copies, waits for them, and re-layouts  2.26 us

profile of v4, /device:TPU:1, one launch (start us, length us, event | category | flops | bytes accessed | tf_op | source)
XLA Modules:
  0.0 62.4 jit_solution(17689221300339508618)
XLA Ops:
  0.0 60.1 %shard_map.82 = bf16[64,8192]{1,0:T(8,128)(2,1)} custom-call(bf16[64,12288]{1,0:T(8,128)(2,1)} %q_any.1, bf16[64,768]{1,0:T(8,128)(2,1)} %kr.1, bf16[64,512]{1,0:T(8,128)(2,1)} %vr.1, bf16[64,128]{1,0:T(8,128)(2,1)} %gates.1, bf16[4,32,192]{2,1,0:T(8,128)(2,1)} %kmix.1, bf16[4,192,192]{2,1,0:T(8,128)(2,1)} %kproj.1, bf16[4,32,128]{2,1,0:T(8,128)(2,1)} %vmix.1, ...), custom_call_target="tpu_custom_call" | custom-call | flops 10000000000 | bytes 10000000 | tf_op jit(solution)/shard_map/pallas_call | solution.py:486
  60.2 2.3 %copy.10 = bf16[64,8192]{1,0:T(8,128)(2,1)} copy(bf16[64,8192]{1,0:T(8,128)(2,1)} %shard_map.82) | data formatting | bytes 2097152

commit v5 on v4

--- a/solution.py
+++ b/solution.py
@@ -68,6 +68,11 @@
     def earlier(act):
         loop(0, (z + 1 - par) // 2, lambda i: act(z - 2 * i - 2 + (1 - par)))
 
+    def await_planes(lower, upper):
+        loop(lower, upper, lambda i: z_copy(z - 2 * i - 2 + (1 - par), z).wait_recv())
+
+    near_planes = (z % 8 + 1 - par) // 2
+
     earlier(lambda zz: greet((zz * 8 + y * 2 + c, x)))
 
     def run_before(k):
@@ -156,7 +161,7 @@
         return remote(own.at[h], win.at[h, slot], win_s.at[h, nxt, x_to], win_r.at[slot], device)
 
     def win_targets(act):
-        for nxt in range(2):
+        for nxt in (1, 0):
             for m in range(4 - 3 * nxt):
                 x_to = (x + m) % 4
                 slot = unit - (8 * (row + nxt) + x_to - 8)
@@ -281,7 +286,7 @@
             win_wait(4 * k)
             passes(k, lambda copy: copy.start())
 
-    earlier(lambda zz: z_copy(zz, z).wait_recv())
+    await_planes(0, near_planes)
 
     def peer(along_x, d):
         if along_x:
@@ -328,7 +333,13 @@
             b_copy(ci, d, *back(ci % 2 == 1, d)).wait_recv()
         d_copy(ci, c).start()
 
-    chunks((3, 2, 1, 0), send_a)
+    @pl.when(z >= 8)
+    def _():
+        chunks((3, 2), send_a)
+
+    @pl.when(z < 8)
+    def _():
+        chunks((1, 0), send_a)
 
     def win_rest(s):
         @pl.when(jnp.logical_and(s != 0, s != 4))
@@ -429,6 +440,8 @@
 
     win_half(c)
     nearest(send_b)
+    await_planes(near_planes, (z + 1 - par) // 2)
+    farther(send_a)
     relay(1 - c, c).wait_recv()
     win_half(1 - c)
     nearest(send_d)

time: 63.6 us -> 63.3 us (level)
  no operation moved by 1% of the time
where the time goes in v5:
time: 63.3 us; the launch traced here: 62.4 us
  Pallas kernels  60.1 us (95%)
  local copies, waits for them, and re-layouts  2.26 us (4%)
    pallas_call x1, Pallas kernels, local(): pl.pallas_call(fused_kernel, out_shape=jax.ShapeDtypeStruct((64, 8192), B...  60.1 us
    unnamed x1, local copies, waits for them, and re-layouts  2.26 us

profile of v5, /device:TPU:1, one launch (start us, length us, event | category | flops | bytes accessed | tf_op | source)
XLA Modules:
  0.0 62.4 jit_solution(17061366525271605996)
XLA Ops:
  0.0 60.1 %shard_map.82 = bf16[64,8192]{1,0:T(8,128)(2,1)} custom-call(bf16[64,12288]{1,0:T(8,128)(2,1)} %q_any.1, bf16[64,768]{1,0:T(8,128)(2,1)} %kr.1, bf16[64,512]{1,0:T(8,128)(2,1)} %vr.1, bf16[64,128]{1,0:T(8,128)(2,1)} %gates.1, bf16[4,32,192]{2,1,0:T(8,128)(2,1)} %kmix.1, bf16[4,192,192]{2,1,0:T(8,128)(2,1)} %kproj.1, bf16[4,32,128]{2,1,0:T(8,128)(2,1)} %vmix.1, ...), custom_call_target="tpu_custom_call" | custom-call | flops 10000000000 | bytes 10000000 | tf_op jit(solution)/shard_map/pallas_call | solution.py:499
  60.1 2.3 %copy.10 = bf16[64,8192]{1,0:T(8,128)(2,1)} copy(bf16[64,8192]{1,0:T(8,128)(2,1)} %shard_map.82) | data formatting | bytes 2097152

commit v6 on v5

--- a/solution.py
+++ b/solution.py
@@ -341,6 +341,24 @@
     def _():
         chunks((1, 0), send_a)
 
+    def nearest(act):
+        @pl.when(z >= 8)
+        def _():
+            chunks((3, 2), act)
+
+        @pl.when(z < 8)
+        def _():
+            chunks((1, 0), act)
+
+    def farther(act):
+        @pl.when(z >= 8)
+        def _():
+            chunks((1, 0), act)
+
+    nearest(send_b)
+    await_planes(near_planes, (z + 1 - par) // 2)
+    farther(send_a)
+
     def win_rest(s):
         @pl.when(jnp.logical_and(s != 0, s != 4))
         def _():
@@ -421,27 +439,10 @@
         run_half(h, KC, lambda hh, odd: comp_keys(hh, odd, chunk),
                  lambda s, g, t: comp_done(s, g, t, first))
 
-    def nearest(act):
-        @pl.when(z >= 8)
-        def _():
-            chunks((3, 2), act)
-
-        @pl.when(z < 8)
-        def _():
-            chunks((1, 0), act)
-
-    def farther(act):
-        @pl.when(z >= 8)
-        def _():
-            chunks((1, 0), act)
-
     def wait_d(ci):
         d_copy(ci, 1 - c).wait_recv()
 
     win_half(c)
-    nearest(send_b)
-    await_planes(near_planes, (z + 1 - par) // 2)
-    farther(send_a)
     relay(1 - c, c).wait_recv()
     win_half(1 - c)
     nearest(send_d)

time: 63.3 us -> 62.6 us (0.989)
  the two profiles are of different devices: /device:TPU:1 before, /device:TPU:480 now
where the time goes in v6:
time: 62.6 us; the launch traced here: 62.4 us
  Pallas kernels  60.2 us (96%)
  local copies, waits for them, and re-layouts  2.26 us (4%)
    pallas_call x1, Pallas kernels, local(): pl.pallas_call(fused_kernel, out_shape=jax.ShapeDtypeStruct((64, 8192), B...  60.2 us
    unnamed x1, local copies, waits for them, and re-layouts  2.26 us

profile of v6, /device:TPU:480, one launch (start us, length us, event | category | flops | bytes accessed | tf_op | source)
XLA Modules:
  0.0 62.4 jit_solution(17369533211418657723)
XLA Ops:
  0.0 60.2 %shard_map.82 = bf16[64,8192]{1,0:T(8,128)(2,1)} custom-call(bf16[64,12288]{1,0:T(8,128)(2,1)} %q_any.1, bf16[64,768]{1,0:T(8,128)(2,1)} %kr.1, bf16[64,512]{1,0:T(8,128)(2,1)} %vr.1, bf16[64,128]{1,0:T(8,128)(2,1)} %gates.1, bf16[4,32,192]{2,1,0:T(8,128)(2,1)} %kmix.1, bf16[4,192,192]{2,1,0:T(8,128)(2,1)} %kproj.1, bf16[4,32,128]{2,1,0:T(8,128)(2,1)} %vmix.1, ...), custom_call_target="tpu_custom_call" | custom-call | flops 10000000000 | bytes 10000000 | tf_op jit(solution)/shard_map/pallas_call | solution.py:500
  60.2 2.3 %copy.10 = bf16[64,8192]{1,0:T(8,128)(2,1)} copy(bf16[64,8192]{1,0:T(8,128)(2,1)} %shard_map.82) | data formatting | bytes 2097152
